TPU v7x, 256 devices: a whole 4x4x8 slice. The times are simulated.
256 devices in a mesh: genome: 64 (over y, z_lo, x), maps: 4 (over z_hi, core).
Axes of the slice: x: 4, y: 4, z: 8 (z_hi: 2, z_lo: 4; z = z_hi * 4 + z_lo), core: 2. Of those that a mesh axis runs over, the one named last changes fastest.
Arguments:
- band_maps: bfloat16 [512, 32, 16384], P('maps', None, 'genome'), may hold values from -300 to 300
- stratum_ids: int32 [16], replicated, may hold values from 4 to 27, as said below
- half_width: int32 [16], replicated, may hold values from 1 to 2
Outputs:
- gram: float32 [512, 16, 512], P('genome', None, 'maps')
- scc: float32 [512, 512], P('genome', 'maps')
Inputs may be any that keep to these rules, and one draw needn't show every extreme that they name: `stratum_ids`: distinct offsets.
All inputs are finite; a program needn't handle non-finite values.
Results may differ from a plain program's by a relative error of at most 0.0003.
Values may be sent and summed in bfloat16 or wider, within the bound.
No kernel may reach another device: no remote copies, remote signals or barrier semaphores. Data moves between devices by JAX's collectives and lax.ppermute only.
A program may use at most 64 MiB of HBM per device.

v0:
```python
import jax
import jax.numpy as jnp
from jax import lax
from jax.sharding import PartitionSpec as P

HMAX = 2


def padded_2(block, sides, width):
    for axis, dim in sides:
        count = lax.axis_size(axis)
        forward = [(i, i + 1) for i in range(count - 1)]
        backward = [(target, source) for source, target in forward]
        low = lax.ppermute(
            lax.slice_in_dim(block, block.shape[dim] - width, None, axis=dim), axis, forward
        )
        high = lax.ppermute(lax.slice_in_dim(block, 0, width, axis=dim), axis, backward)
        block = jnp.concatenate([low, block, high], axis=dim)
    return block


def body(band_maps, stratum_ids, half_width):
    genome_size = lax.axis_size("genome")
    panel_maps = band_maps.shape[0]
    bin_count = band_maps.shape[2]
    strata_count = stratum_ids.shape[0]
    total_bins = bin_count * genome_size
    maps_total = panel_maps * lax.axis_size("maps")
    padded = padded_2(band_maps, (("genome", 2),), HMAX)
    weights = [
        (jnp.abs(jnp.int32(lag)) <= half_width).astype(jnp.float32)
        for lag in range(-HMAX, HMAX + 1)
    ]
    window = (2 * half_width + 1).astype(jnp.float32)
    smooth = jnp.zeros((panel_maps, strata_count, bin_count), jnp.float32)
    for lag_rows in range(-2 * HMAX, 2 * HMAX + 1):
        picked = jnp.take(padded, stratum_ids + lag_rows, axis=1)
        for across in range(-HMAX, HMAX + 1):
            along = across + lag_rows
            if abs(along) <= HMAX:
                factor = (weights[across + HMAX] * weights[along + HMAX])[None, :, None]
                smooth = smooth + factor * picked[
                    :, :, HMAX + across : HMAX + across + bin_count
                ].astype(jnp.float32)
    smooth = smooth / (window * window)[None, :, None]
    totals = lax.psum(jnp.sum(smooth, axis=2), "genome")
    centre = totals / total_bins
    deviation = smooth - centre[:, :, None]
    spread = lax.psum(jnp.sum(deviation * deviation, axis=2), "genome") / total_bins
    spread_all = lax.all_gather(spread, "maps", axis=0, tiled=True)
    centered = deviation.astype(jnp.bfloat16)
    rows_dev = maps_total // genome_size
    product_block = jnp.einsum(
        "akb,mkb->akm",
        lax.all_gather(centered, "maps", axis=0, tiled=True),
        centered,
        preferred_element_type=jnp.float32,
    )
    tile_sum = lax.psum_scatter(product_block, "genome", scatter_dimension=0, tiled=True)
    gram = tile_sum / total_bins
    row_start = lax.axis_index("genome") * rows_dev
    spread_rows = lax.dynamic_slice_in_dim(spread_all, row_start, rows_dev, 0)
    denominator = jnp.sum(jnp.sqrt(spread_rows[:, :, None] * spread.T[None, :, :]), axis=1)
    scc = jnp.sum(gram, axis=1) / denominator
    return (gram, scc)


def solution(mesh):
    in_specs = (P("maps", None, "genome"), P(), P())
    out_specs = (P("genome", None, "maps"), P("genome", "maps"))
    return jax.shard_map(body, mesh=mesh, in_specs=in_specs, out_specs=out_specs, check_vma=False)
```

profile of v0, /device:TPU:0, one launch (start us, length us, event | category | flops | bytes accessed | tf_op | source)
XLA Modules:
  0.0 708.0 jit_solution(7486554281614843541)
XLA Ops:
  7.2 0.0 copy-start.9
  7.2 0.0 copy-start.10
  7.2 0.0 all-gather.2.cloned.1.call-start
  7.2 3.5 copy.37
  10.7 0.0 copy-start
  10.7 1.7 collective-permute-start
  12.4 1.3 collective-permute-start.1
  13.7 0.0 copy-done.9
  13.9 0.0 copy-done.10
  13.9 0.0 collective-permute-done
  13.9 0.0 copy-done
  13.9 4.1 collective-permute-done.1
  18.0 2.6 pad_maximum_fusion
  20.6 0.8 gather_fusion.5
  21.4 1.5 copy.45
  22.9 0.8 gather_fusion.6
  23.7 1.6 copy.46
  25.3 0.8 gather_fusion.1
  26.0 1.6 copy.41
  27.6 0.8 gather_fusion.2
  28.4 1.6 copy.42
  29.9 0.8 gather_fusion.7
  30.7 1.5 copy.47
  32.2 0.8 gather_fusion.8
  33.0 1.6 copy.48
  34.6 0.8 gather_fusion.3
  35.3 1.6 copy.43
  37.0 0.8 gather_fusion.4
  37.7 1.5 copy.44
  39.3 0.8 gather_fusion
  40.0 0.8 copy.40
  40.9 0.0 copy-start.1
  40.9 0.2 select_bitcast_fusion.8
  41.2 1.1 copy-done.1
  42.3 0.5 copy-done.5
  42.8 0.4 select_bitcast_fusion.2
  43.2 1.0 copy-done.2
  44.2 0.5 copy-done.6
  44.7 0.4 select_bitcast_fusion.6
  45.1 1.0 copy-done.3
  46.1 0.5 copy-done.7
  46.5 0.4 select_bitcast_fusion
  47.0 1.0 copy-done.4
  47.9 0.5 copy-done.8
  48.4 0.4 select_bitcast_fusion.4
  48.8 9.0 %fusion.4 = (f32[128,16]{0,1:T(8,128)S(1)}, f32[128,16,256]{2,0,1:T(8,128)S(1)}) fusion(f32[16]{0:T(128)S(1)} %get-tuple-element.42, bf16[128,16,260]{2,0,1:T(8,128)(2,1)S(1)} %get-tuple-element.59, bf16[128,16,260]{2,0,1:T(8,128)(2,1)S(1)} %get-tuple-element.60, bf16[128,16,260]{2,0,1:T(8,128)(2,1)S(1)} %get-tuple-element.61, ...), kind=kLoop, calls=%fused_computation.67 | loop fusion | flops 39843840 | bytes 28320192 | tf_op jit(solution)/shard_map/reduce_sum | solution.py:46
  57.8 190.7 %psum.14 = f32[128,16]{0,1:T(8,128)S(1)} all-reduce(f32[128,16]{0,1:T(8,128)S(1)} %get-tuple-element.13), channel_id=1, replica_groups=mesh['genome'=64,'maps'=4] {'genome'}, use_global_device_ids=true, to_apply=%region_1.3 | all-reduce | flops 2048 | bytes 16384 | tf_op jit(solution)/shard_map/psum | solution.py:46
  248.5 1.4 multiply_reduce_fusion
  249.9 0.0 all-gather.2.cloned.1.call-update
  249.9 0.0 reduce-scatter.2.cloned.1.call-start
  250.0 61.9 %all-gather.2.cloned.1.call-done = bf16[512,16,256]{2,0,1:T(8,128)(2,1)} async-done(((bf16[128,16,256]{2,0,1:T(8,128)(2,1)}), bf16[512,16,256]{2,0,1:T(8,128)(2,1)}) %all-gather.2.cloned.1.call-update) | async-done | bytes 4194320 | tf_op jit(solution)/shard_map/all_gather | solution.py:55
  311.9 5.9 convolution_bitcast_fusion
  317.8 5.5 copy.49
  323.3 0.0 reduce-scatter.2.cloned.1.call-update
  323.3 186.1 %psum.15 = f32[128,16]{0,1:T(8,128)S(1)} all-reduce(f32[128,16]{0,1:T(8,128)S(1)} %get-tuple-element.31), channel_id=1, replica_groups=mesh['genome'=64,'maps'=4] {'genome'}, use_global_device_ids=true, to_apply=%region_5.7 | all-reduce | flops 2048 | bytes 16384 | tf_op jit(solution)/shard_map/psum | solution.py:49
  509.4 9.1 %all_gather.7 = f32[512,16]{0,1:T(8,128)S(1)} all-gather(f32[128,16]{0,1:T(8,128)S(1)} %get-tuple-element.35), channel_id=1, replica_groups=mesh['genome'=64,'maps'=4] {'maps'}, dimensions={0}, use_global_device_ids=true | all-gather | bytes 40960 | tf_op jit(solution)/shard_map/all_gather | solution.py:50
  518.6 0.1 constant_dynamic-slice_fusion
  518.7 0.1 copy.51
  518.7 0.1 sqrt_reduce_fusion
  518.8 0.1 copy.52
  518.9 179.9 %reduce-scatter.2.cloned.1.call-done = f32[8,16,128]{2,1,0:T(8,128)} async-done(((f32[512,16,128]{2,1,0:T(8,128)}), f32[8,16,128]{2,1,0:T(8,128)}) %reduce-scatter.2.cloned.1.call-update) | async-done | bytes 65552 | tf_op jit(solution)/shard_map/reduce_scatter | solution.py:59
  698.9 1.5 fusion.3
  700.4 0.1 copy.54
  700.5 0.7 copy.53
  (23 shorter events, 0.2 us)
Async XLA Ops:
  7.2 6.6 copy-start.9
  7.2 6.7 copy-start.10
  7.2 304.7 %all-gather.2.cloned.1.call-start = ((), (), s32[]{:S(2)}) async-start(), calls=%async_computation.1 | async-start | bytes 5242880 | tf_op jit(solution)/shard_map/all_gather | solution.py:55
  10.7 3.2 copy-start
  10.7 3.2 collective-permute-start
  12.4 5.6 collective-permute-start.1
  40.9 1.4 copy-start.1
  40.9 1.9 copy-start.5
  42.8 1.4 copy-start.2
  42.8 1.9 copy-start.6
  44.7 1.4 copy-start.3
  44.7 1.9 copy-start.7
  46.5 1.4 copy-start.4
  46.5 1.9 copy-start.8
  249.9 449.0 %reduce-scatter.2.cloned.1.call-start = ((), (), s32[]{:S(2)}) async-start(), calls=%async_computation.2 | async-start | bytes 4259840 | tf_op jit(solution)/shard_map/reduce_scatter | solution.py:59
Sparse Core Ops, SparseCore 0:
  250.0 61.7 all-gather.1
  323.4 375.4 reduce-scatter.1
where the time goes:
time: 708 us
  blocking collectives  386 us (55%)
  waiting for transfers between devices  246 us (35%)
  local copies, waits for them, and re-layouts  36.1 us (5%)
  other arithmetic  16.5 us (2%)
  between operations  14.4 us (2%)
    psum x1, blocking collectives, body(): totals = lax.psum(jnp.sum(smooth, axis=2), 'genome')  191 us
    psum x1, blocking collectives, body(): lax.psum(jnp.sum(deviation * deviation, axis=2), 'genome') / total_bins  186 us
    reduce_scatter x1, waiting for transfers between devices, body(): lax.psum_scatter(product_block, 'genome', scatter_dimension=0, tiled=True)  180 us
    all_gather x1, waiting for transfers between devices, body(): lax.all_gather(centered, 'maps', axis=0, tiled=True)  61.9 us
    gather x18, local copies, waits for them, and re-layouts, body(): picked = jnp.take(padded, stratum_ids + lag_rows, axis=1)  20.2 us
  transfers between devices with their start and end apart: 4, of which 3 were waited for; matrix products, arithmetic and copies ran while one was open for 0% of the time, Pallas kernels for 0%

commit v1 on v0

v1 whole, which is shorter than its diff:
```python
import jax
import jax.numpy as jnp
from jax import lax
from jax.experimental import pallas as pl
from jax.experimental.pallas import tpu as pltpu
from jax.sharding import Mesh, PartitionSpec as P

HMAX = 2
BINS_AXES = ("y", "zl", "x")
MAPS_AXES = ("zh", "core")
STRATA_AXES = ("zl", "zh", "core")
SUM_AXES = ("y", "x")
F32 = jnp.float32
BF16 = jnp.bfloat16
HEAD = 8
VMEM_LIMIT = 32 * 1024 * 1024


def params():
    return pltpu.CompilerParams(vmem_limit_bytes=VMEM_LIMIT)


def edge_kernel(band_ref, edge_ref):
    maps, wide, bins = band_ref.shape
    rows = maps * wide
    data = band_ref[...].reshape(rows, bins)
    column = lax.broadcasted_iota(jnp.int32, (bins, 128), 0)
    part = lax.rem(lax.broadcasted_iota(jnp.int32, (bins, 128), 1), 4)
    pick = (column == jnp.where(part < 2, bins - 2 + part, part - 2)).astype(BF16)
    spread = jnp.dot(data, pick, preferred_element_type=F32).reshape(maps, wide, 128)
    offset = lax.broadcasted_iota(jnp.int32, (wide, 128), 0)
    lane = lax.broadcasted_iota(jnp.int32, (wide, 128), 1)
    spread = jnp.where((lax.div(lane, 4) == offset)[None], spread, 0.0)
    spread = spread.astype(BF16).reshape(rows, 128)
    m = lax.broadcasted_iota(jnp.int32, (maps, rows), 0)
    r = lax.broadcasted_iota(jnp.int32, (maps, rows), 1)
    gather = (lax.div(r, wide) == m).astype(BF16)
    edge_ref[...] = jnp.dot(gather, spread, preferred_element_type=F32).astype(BF16)


def edges(band_maps):
    maps, wide, bins = band_maps.shape
    step = 32
    return pl.pallas_call(
        edge_kernel,
        grid=(maps // step,),
        in_specs=[pl.BlockSpec((step, wide, bins), lambda i: (i, 0, 0))],
        out_specs=pl.BlockSpec((step, 128), lambda i: (i, 0)),
        out_shape=jax.ShapeDtypeStruct((maps, 128), BF16),
        compiler_params=params(),
        name="edges",
    )(band_maps)


def smooth_kernel(ids_ref, half_ref, band_ref, low_ref, high_ref, out_ref, plane_ref, turned_ref, win_ref, perm_ref):
    maps, wide, bins = band_ref.shape
    strata = out_ref.shape[0]
    r = lax.broadcasted_iota(jnp.int32, (8 * wide, 8 * wide), 0)
    c = lax.broadcasted_iota(jnp.int32, (8 * wide, 8 * wide), 1)
    perm_ref[...] = (c == lax.rem(r, 8) * wide + lax.div(r, 8)).astype(BF16)
    for g in range(maps // 8):
        group = jnp.dot(
            perm_ref[...], band_ref[pl.ds(8 * g, 8)].reshape(8 * wide, bins), preferred_element_type=F32
        )
        plane_ref[:, pl.ds(8 * g, 8), :] = group.reshape(wide, 8, bins)

    low = jnp.transpose(low_ref[...].astype(F32))
    high = jnp.transpose(high_ref[...].astype(F32))
    for d in range(wide):
        turned_ref[d, pl.ds(HEAD - 2, 2), :] = low[4 * d : 4 * d + 2, :]
        turned_ref[d, pl.ds(HEAD + bins, 2), :] = high[4 * d + 2 : 4 * d + 4, :]

    def turn(d, carry):
        for half in range(bins // 128):
            tile = plane_ref[d, :, half * 128 : half * 128 + 128]
            turned_ref[d, pl.ds(HEAD + half * 128, 128), :] = jnp.transpose(tile)
        return carry

    lax.fori_loop(0, wide, turn, 0, unroll=4)

    def windows(i, carry):
        rows = pl.ds(pl.multiple_of(i * 16, 16), 16)
        planes = [turned_ref[d, rows, :] for d in range(wide)]
        for mid in range(1, wide - 1):
            one = planes[mid - 1] + planes[mid] + planes[mid + 1]
            win_ref[0, mid, rows, :] = one
            if 2 <= mid < wide - 2:
                win_ref[1, mid, rows, :] = one + (planes[mid - 2] + planes[mid + 2])
        return carry

    lax.fori_loop(0, turned_ref.shape[1] // 16, windows, 0)

    row = lax.broadcasted_iota(jnp.int32, (16, maps), 0)
    step = 64

    def stratum(k, carry):
        wider = half_ref[k] >= 2
        h = jnp.where(wider, 1, 0)
        reach = jnp.where(wider, 2, 0)
        outer = jnp.where(wider, 1.0, 0.0)
        scale = jnp.where(wider, 1.0 / 25.0, 1.0 / 9.0)
        centre = ids_ref[k]
        parts = []
        total = jnp.zeros((1, maps), F32)
        for i in range(bins // step):
            at = HEAD + i * step
            acc = win_ref[h, centre, pl.ds(at, step), :]
            acc = acc + win_ref[h, centre + 1, pl.ds(at - 1, step), :]
            acc = acc + win_ref[h, centre - 1, pl.ds(at + 1, step), :]
            far = win_ref[h, centre + reach, pl.ds(at - 2, step), :] + win_ref[h, centre - reach, pl.ds(at + 2, step), :]
            acc = (acc + far * outer) * scale
            parts.append(acc)
            total = total + jnp.sum(acc, axis=0, keepdims=True)
        mean = total * (1.0 / bins)
        for i, acc in enumerate(parts):
            out_ref[k, pl.ds(i * step, step), :] = (acc - mean).astype(BF16)
        hi = mean.astype(BF16).astype(F32)
        mid = (mean - hi).astype(BF16).astype(F32)
        low = mean - hi - mid
        side = jnp.where(row == 0, hi, jnp.where(row == 1, mid, jnp.where(row == 2, low, 0.0)))
        out_ref[k, pl.ds(bins, 16), :] = side.astype(BF16)
        return carry

    lax.fori_loop(0, strata, stratum, 0, unroll=2)


def smoothed(band_maps, low, high, stratum_ids, half_width):
    maps, wide, bins = band_maps.shape
    strata = stratum_ids.shape[0]
    rows = bins + 16
    smem = pl.BlockSpec(memory_space=pltpu.SMEM)
    vmem = pl.BlockSpec(memory_space=pltpu.VMEM)
    return pl.pallas_call(
        smooth_kernel,
        in_specs=[smem, smem, vmem, vmem, vmem],
        out_specs=vmem,
        out_shape=jax.ShapeDtypeStruct((strata, rows, 128), BF16),
        scratch_shapes=[
            pltpu.VMEM((wide, maps, bins), F32),
            pltpu.VMEM((wide, bins + 2 * HEAD, maps), F32),
            pltpu.VMEM((2, wide, bins + 2 * HEAD, maps), F32),
            pltpu.VMEM((8 * wide, 8 * wide), BF16),
        ],
        compiler_params=params(),
        name="smooth",
    )(stratum_ids, half_width, band_maps, low, high)


def dot_tn(a, b):
    return lax.dot_general(
        a, b, (((0,), (0,)), ((), ())), precision=lax.Precision.HIGHEST, preferred_element_type=F32
    )


def gram_kernel(blocks, panels, sum_y, sum_x, bins, in_ref, out_ref, data_ref, mean_ref, gram_ref):
    maps = 128
    total = panels * maps
    mean_ref[...] = jnp.zeros_like(mean_ref)
    for z in range(blocks):
        for m in range(panels):
            src = z * panels + m
            data_ref[pl.ds(z * bins, bins), pl.ds(m * maps, maps)] = in_ref[src, pl.ds(0, bins), :]
            words = in_ref[src, pl.ds(bins, 16), :].astype(F32)
            mean_ref[z : z + 1, m * maps : (m + 1) * maps] = words[0:1] + words[1:2] + words[2:3]
    means = mean_ref[...]
    centre = jnp.sum(means, axis=0, keepdims=True) * (1.0 / blocks)
    row = lax.broadcasted_iota(jnp.int32, means.shape, 0)
    dev = jnp.where(row < blocks, means - centre, 0.0)
    data = data_ref[...]
    gram_ref[...] = lax.dot_general(
        data, data, (((0,), (0,)), ((), ())), preferred_element_type=F32
    ) + dot_tn(dev, dev) * float(bins)
    r = lax.broadcasted_iota(jnp.int32, (maps, maps), 0)
    c = lax.broadcasted_iota(jnp.int32, (maps, maps), 1)
    side = [centre[:, m * maps : (m + 1) * maps] for m in range(panels)]
    for m in range(panels):
        block = gram_ref[pl.ds(m * maps, maps), pl.ds(m * maps, maps)]
        side.append(jnp.sum(jnp.where(r == c, block, 0.0), axis=0, keepdims=True))
    side = jnp.concatenate(side, axis=0)
    per = maps // (blocks * sum_x)
    for y in range(sum_y):
        for x in range(sum_x):
            d = y * sum_x + x
            for m in range(panels):
                for z in range(blocks):
                    q = y * maps + (z * sum_x + x) * per
                    out_ref[d, pl.ds((m * blocks + z) * per, per), :] = gram_ref[
                        pl.ds(q, per), pl.ds(m * maps, maps)
                    ]
            out_ref[d, pl.ds(panels * blocks * per, 2 * panels), :] = side


def partial_gram(received, blocks, panels, sum_y, sum_x):
    bins = received.shape[1] - 16
    total = panels * 128
    per = 128 // (blocks * sum_x)
    vmem = pl.BlockSpec(memory_space=pltpu.VMEM)
    return pl.pallas_call(
        lambda *refs: gram_kernel(blocks, panels, sum_y, sum_x, bins, *refs),
        in_specs=[vmem],
        out_specs=vmem,
        out_shape=jax.ShapeDtypeStruct(
            (sum_y * sum_x, panels * blocks * per + 2 * panels, 128), F32
        ),
        scratch_shapes=[
            pltpu.VMEM((blocks * bins, total), BF16),
            pltpu.VMEM((8, total), F32),
            pltpu.VMEM((total, total), F32),
        ],
        compiler_params=params(),
        name="partial_gram",
    )(received)


def sum_kernel(blocks, panels, sum_x, count, in_ref, out_ref, mean_ref, between_ref, spread_ref):
    maps = 128
    parts = in_ref.shape[0]
    rows = in_ref.shape[1] - 2 * panels
    per = rows // (panels * blocks)
    total_bins = float(count * parts)
    for m in range(panels):
        mean_ref[:, m * maps : (m + 1) * maps] = jnp.concatenate(
            [in_ref[d, pl.ds(rows + m, 1), :] for d in range(parts)], axis=0
        )
    means = mean_ref[...]
    dev = means - jnp.sum(means, axis=0, keepdims=True) * (1.0 / parts)
    own = jnp.concatenate(
        [
            sum(in_ref[d, pl.ds(rows + panels + m, 1), :] for d in range(parts))
            for m in range(panels)
        ],
        axis=1,
    )
    spread = (own + float(count) * jnp.sum(dev * dev, axis=0, keepdims=True)) * (1.0 / total_bins)
    y = lax.axis_index("y")
    x = lax.axis_index("x")
    for m in range(panels):

        @pl.when(y == m)
        def _():
            cols = slice(m * maps, (m + 1) * maps)
            between_ref[...] = dot_tn(dev[:, cols], dev) * float(count)
            spread_ref[...] = jnp.transpose(jnp.broadcast_to(spread[:, cols], (maps, maps)))

    for z in range(blocks):
        start = pl.multiple_of((z * sum_x + x) * per, per)
        between = between_ref[pl.ds(start, per), :]
        spread_q = spread_ref[pl.ds(start, per), :]
        for m in range(panels):
            tile = pl.ds((m * blocks + z) * per, per)
            acc = in_ref[0, tile, :]
            for d in range(1, parts):
                acc = acc + in_ref[d, tile, :]
            cols = slice(m * maps, (m + 1) * maps)
            out_ref[z * panels + m, pl.ds(0, per), :] = (acc + between[:, cols]) * (1.0 / total_bins)
            out_ref[z * panels + m, pl.ds(per, per), :] = jnp.sqrt(spread_q * spread[:, cols])


def summed(received, blocks, panels, sum_x, count):
    parts = received.shape[0]
    per = (received.shape[1] - 2 * panels) // (panels * blocks)
    vmem = pl.BlockSpec(memory_space=pltpu.VMEM)
    return pl.pallas_call(
        lambda *refs: sum_kernel(blocks, panels, sum_x, count, *refs),
        in_specs=[vmem],
        out_specs=vmem,
        out_shape=jax.ShapeDtypeStruct((blocks * panels, 2 * per, 128), F32),
        scratch_shapes=[
            pltpu.VMEM((parts, panels * 128), F32),
            pltpu.VMEM((128, panels * 128), F32),
            pltpu.VMEM((128, 128), F32),
        ],
        compiler_params=params(),
        name="sum_parts",
    )(received)


def final_kernel(in_ref, gram_ref, scc_ref):
    strata, rows, _ = in_ref.shape
    per = rows // 2
    top = jnp.zeros((per, 128), F32)
    bottom = jnp.zeros((per, 128), F32)
    for k in range(strata):
        tile = in_ref[k, pl.ds(0, per), :]
        gram_ref[:, k, :] = tile
        top = top + tile
        bottom = bottom + in_ref[k, pl.ds(per, per), :]
    scc_ref[...] = top / bottom


def final(received):
    strata, rows, lanes = received.shape
    vmem = pl.BlockSpec(memory_space=pltpu.VMEM)
    return pl.pallas_call(
        final_kernel,
        in_specs=[vmem],
        out_specs=[vmem, vmem],
        out_shape=[
            jax.ShapeDtypeStruct((rows // 2, strata, lanes), F32),
            jax.ShapeDtypeStruct((rows // 2, lanes), F32),
        ],
        compiler_params=params(),
        name="final",
    )(received)


def body(band_maps, stratum_ids, half_width):
    maps, wide, bins = band_maps.shape
    blocks, sum_y, sum_x = (lax.axis_size(a) for a in ("zl", "y", "x"))
    panels = lax.axis_size(MAPS_AXES)
    genome = lax.axis_size(BINS_AXES)
    edge = edges(band_maps)
    forward = [(i, i + 1) for i in range(genome - 1)]
    backward = [(i + 1, i) for i in range(genome - 1)]
    low = lax.ppermute(edge, BINS_AXES, forward)
    high = lax.ppermute(edge, BINS_AXES, backward)
    strata = smoothed(band_maps, low, high, stratum_ids, half_width)
    strata = lax.all_to_all(strata, STRATA_AXES, 0, 0, tiled=True)
    parts = partial_gram(strata, blocks, panels, sum_y, sum_x)
    parts = lax.all_to_all(parts, SUM_AXES, 0, 0, tiled=True)
    tiles = summed(parts, blocks, panels, sum_x, blocks * bins)
    tiles = lax.all_to_all(tiles, STRATA_AXES, 0, 0, tiled=True)
    gram, scc = final(tiles)
    return gram, scc


def solution(mesh):
    split = Mesh(mesh.devices.reshape(4, 4, 4, 2, 2), BINS_AXES + MAPS_AXES)
    in_specs = (P(MAPS_AXES, None, BINS_AXES), P(), P())
    out_specs = (P(BINS_AXES, None, MAPS_AXES), P(BINS_AXES, MAPS_AXES))
    return jax.shard_map(body, mesh=split, in_specs=in_specs, out_specs=out_specs, check_vma=False)
```

time: 708 us -> 103 us (0.15)
  the two profiles are of different devices: /device:TPU:0 before, /device:TPU:1 now
where the time goes in v1:
time: 103 us
  blocking collectives  84.2 us (82%)
  Pallas kernels  9.35 us (9%)
  starting transfers between devices  5.86 us (6%)
  local copies, waits for them, and re-layouts  1.59 us (2%)
    all_to_all x1, blocking collectives, body(): strata = lax.all_to_all(strata, STRATA_AXES, 0, 0, tiled=True)  45.7 us
    all_to_all x1, blocking collectives, body(): parts = lax.all_to_all(parts, SUM_AXES, 0, 0, tiled=True)  25.9 us
    all_to_all x1, blocking collectives, body(): tiles = lax.all_to_all(tiles, STRATA_AXES, 0, 0, tiled=True)  12.6 us
    ppermute x1, starting transfers between devices, body(): low = lax.ppermute(edge, BINS_AXES, forward)  4.57 us
    pallas_call x1, Pallas kernels, smoothed(): pl.pallas_call(smooth_kernel, in_specs=[smem, smem, vmem, vmem, vmem], ou...  4.56 us
  transfers between devices with their start and end apart: 2, of which 1 were waited for; matrix products, arithmetic and copies ran while one was open for 0% of the time, Pallas kernels for 0%

profile of v1, /device:TPU:1, one launch (start us, length us, event | category | flops | bytes accessed | tf_op | source)
XLA Modules:
  0.0 102.7 jit_solution(5234889556505012075)
XLA Ops:
  0.6 0.0 copy-start
  0.6 1.6 %copy-done = bf16[128,32,256]{2,1,0:T(8,128)(2,1)S(1)} copy-done((bf16[128,32,256]{2,1,0:T(8,128)(2,1)S(1)}, bf16[128,32,256]{2,1,0:T(8,128)(2,1)}, u32[]{:S(2)}) %copy-start) | copy-done | bytes 2097176
  2.2 0.0 copy-start.1
  2.2 0.0 copy-start.2
  2.2 1.9 %edges.1 = bf16[128,128]{1,0:T(8,128)(2,1)S(1)} custom-call(bf16[128,32,256]{2,1,0:T(8,128)(2,1)S(1)} %copy-done), custom_call_target="tpu_custom_call" | custom-call | tf_op jit(solution)/shard_map/edges/pallas_call | solution.py:44
  4.1 1.3 %collective-permute-start.1 = (bf16[128,128]{1,0:T(8,128)(2,1)S(1)}, bf16[128,128]{1,0:T(8,128)(2,1)S(1)}, u32[]{:S(2)}, u32[]{:S(2)}) collective-permute-start(bf16[128,128]{1,0:T(8,128)(2,1)S(1)} %edges.1), channel_id=1, source_target_pairs={{4,0},{8,4},{12,8},{16,12},{20,16},{24,20},{28,24},{32,28},{36,32}... | collective-permute-start | bytes 98312 | tf_op jit(solution)/shard_map/ppermute | solution.py:316
  5.4 4.6 %collective-permute-start = (bf16[128,128]{1,0:T(8,128)(2,1)S(1)}, bf16[128,128]{1,0:T(8,128)(2,1)S(1)}, u32[]{:S(2)}, u32[]{:S(2)}) collective-permute-start(bf16[128,128]{1,0:T(8,128)(2,1)S(1)} %edges.1), channel_id=1, source_target_pairs={{0,4},{4,8},{8,12},{12,16},{16,20},{20,24},{24,28},{28,32},{32,36}... | collective-permute-start | bytes 98312 | tf_op jit(solution)/shard_map/ppermute | solution.py:315
  10.0 0.0 collective-permute-done.1.high_ref
  10.0 1.0 collective-permute-done.low_ref
  11.0 0.0 copy-done.1
  11.0 0.0 copy-done.2
  11.0 4.6 %smooth.1 = bf16[16,272,128]{2,1,0:T(8,128)(2,1)S(1)} custom-call(s32[16]{0:T(128)S(1)} %copy-done.1, s32[16]{0:T(128)S(1)} %copy-done.2, bf16[128,32,256]{2,1,0:T(8,128)(2,1)S(1)} %copy-done, bf16[128,128]{1,0:T(8,128)(2,1)S(1)} %collective-permute-done.low_ref, bf16[128,128]{1,0:T(8,128)(2,1)S(1)} %collective-permute-done.1.high_ref), custom_call_target="tpu_custom_call" | custom-call | tf_op jit(solution)/shard_map/smooth/pallas_call | solution.py:133
  15.6 45.7 %all_to_all.15.refs_0_ = bf16[16,272,128]{2,1,0:T(8,128)(2,1)S(1)} all-to-all(bf16[16,272,128]{2,1,0:T(8,128)(2,1)S(1)} %smooth.1), channel_id=1, replica_groups=mesh['y'=4,'zl'=4,'x'=4,'zh'=2,'core'=2] {'zl','zh','core'}, dimensions={0} | all-to-all | bytes 2228224 | tf_op jit(solution)/shard_map/all_to_all | solution.py:318
  61.3 1.7 %partial_gram.1 = f32[16,136,128]{2,1,0:T(8,128)S(1)} custom-call(bf16[16,272,128]{2,1,0:T(8,128)(2,1)S(1)} %all_to_all.15.refs_0_), custom_call_target="tpu_custom_call" | custom-call | tf_op jit(solution)/shard_map/partial_gram/pallas_call | solution.py:198
  63.0 25.9 %all_to_all.16.refs_0_ = f32[16,136,128]{2,1,0:T(8,128)S(1)} all-to-all(f32[16,136,128]{2,1,0:T(8,128)S(1)} %partial_gram.1), channel_id=1, replica_groups=mesh['y'=4,'zl'=4,'x'=4,'zh'=2,'core'=2] {'y','x'}, dimensions={0} | all-to-all | bytes 2228224 | tf_op jit(solution)/shard_map/all_to_all | solution.py:320
  88.9 0.5 sum_parts.1
  89.4 12.6 %all_to_all.17.in_ref = f32[16,16,128]{2,1,0:T(8,128)S(1)} all-to-all(f32[16,16,128]{2,1,0:T(8,128)S(1)} %sum_parts.1), channel_id=1, replica_groups=mesh['y'=4,'zl'=4,'x'=4,'zh'=2,'core'=2] {'zl','zh','core'}, dimensions={0} | all-to-all | bytes 262144 | tf_op jit(solution)/shard_map/all_to_all | solution.py:322
  102.0 0.7 final.1
Async XLA Ops:
  0.6 1.6 %copy-start = (bf16[128,32,256]{2,1,0:T(8,128)(2,1)S(1)}, bf16[128,32,256]{2,1,0:T(8,128)(2,1)}, u32[]{:S(2)}) copy-start(bf16[128,32,256]{2,1,0:T(8,128)(2,1)} %band_ref.3) | copy-start | bytes 6291460
  2.2 8.8 %copy-start.1 = (s32[16]{0:T(128)S(1)}, s32[16]{0:T(128)}, u32[]{:S(2)}) copy-start(s32[16]{0:T(128)} %ids_ref.1) | copy-start | bytes 196
  2.2 8.8 %copy-start.2 = (s32[16]{0:T(128)S(1)}, s32[16]{0:T(128)}, u32[]{:S(2)}) copy-start(s32[16]{0:T(128)} %half_ref.1) | copy-start | bytes 196
  4.1 5.9 %collective-permute-start.1 = (bf16[128,128]{1,0:T(8,128)(2,1)S(1)}, bf16[128,128]{1,0:T(8,128)(2,1)S(1)}, u32[]{:S(2)}, u32[]{:S(2)}) collective-permute-start(bf16[128,128]{1,0:T(8,128)(2,1)S(1)} %edges.1), channel_id=1, source_target_pairs={{4,0},{8,4},{12,8},{16,12},{20,16},{24,20},{28,24},{32,28},{36,32}... | collective-permute-start | bytes 98312 | tf_op jit(solution)/shard_map/ppermute | solution.py:316
  5.4 5.6 %collective-permute-start = (bf16[128,128]{1,0:T(8,128)(2,1)S(1)}, bf16[128,128]{1,0:T(8,128)(2,1)S(1)}, u32[]{:S(2)}, u32[]{:S(2)}) collective-permute-start(bf16[128,128]{1,0:T(8,128)(2,1)S(1)} %edges.1), channel_id=1, source_target_pairs={{0,4},{4,8},{8,12},{12,16},{16,20},{20,24},{24,28},{28,32},{32,36}... | collective-permute-start | bytes 98312 | tf_op jit(solution)/shard_map/ppermute | solution.py:315

commit v2 on v1

v2 whole, which is shorter than its diff:
```python
import jax
import jax.numpy as jnp
from jax import lax
from jax.experimental import pallas as pl
from jax.experimental.pallas import tpu as pltpu
from jax.sharding import Mesh, PartitionSpec as P

HMAX = 2
BINS_AXES = ("y", "zl", "x")
MAPS_AXES = ("zh", "core")
HALO_AXES = ("y", "zl", "x", "zh")
STRATA_AXES = ("zh", "zl", "core")
SUM_AXES = ("x", "y")
F32 = jnp.float32
BF16 = jnp.bfloat16
HALO = 4
TAIL = 8
RIM = 2
SIDE = 2 + 2 * RIM
VMEM_LIMIT = 28 * 1024 * 1024


def place(z, m, blocks, cores):
    return ((m // cores) * blocks + z) * cores + m % cores


def next_to_here():
    _, zl, x, zh = (lax.axis_size(a) for a in HALO_AXES)
    pairs = []
    for y in range(lax.axis_size("y")):
        flat = [((y * zl + p // x % zl) * x + p % x) * zh + p // (x * zl) for p in range(zh * zl * x)]
        pairs += [(flat[(p + 1) % len(flat)], flat[p]) for p in range(len(flat))]
    return pairs


def params():
    return pltpu.CompilerParams(vmem_limit_bytes=VMEM_LIMIT)


def edge_kernel(band_ref, edge_ref, copy_ref, sems):
    maps, wide, bins = band_ref.shape
    parts = sems.shape[1]
    each = maps // parts
    copies = [
        [
            pltpu.make_async_copy(
                band_ref.at[pl.ds(i * each, each), :, pl.ds(first, size)],
                copy_ref.at[pl.ds(i * each, each), :, pl.ds(first, size)],
                sems.at[half, i],
            )
            for i in range(parts)
        ]
        for half, (first, size) in enumerate(((0, 128), (128, bins - 128)))
    ]
    for copy in copies[0] + copies[1]:
        copy.start()
    column = lax.broadcasted_iota(jnp.int32, (128, 128), 0)
    part = lax.rem(lax.broadcasted_iota(jnp.int32, (128, 128), 1), HALO)
    pick = (column == part).astype(BF16)
    offset = lax.broadcasted_iota(jnp.int32, (wide, 128), 0)
    lane = lax.broadcasted_iota(jnp.int32, (wide, 128), 1)
    own = (lax.div(lane, HALO) == offset)[None]
    rows = each * wide
    m = lax.broadcasted_iota(jnp.int32, (each, rows), 0)
    r = lax.broadcasted_iota(jnp.int32, (each, rows), 1)
    gather = (lax.div(r, wide) == m).astype(BF16)
    for i, copy in enumerate(copies[0]):
        copy.wait()
        data = copy_ref[pl.ds(i * each, each), :, pl.ds(0, 128)].reshape(rows, 128)
        spread = jnp.dot(data, pick, preferred_element_type=F32).reshape(each, wide, 128)
        spread = jnp.where(own, spread, 0.0).astype(BF16).reshape(rows, 128)
        edge = jnp.dot(gather, spread, preferred_element_type=F32)
        edge_ref[pl.ds(i * each, each), :] = edge.astype(BF16)
    for copy in copies[1]:
        copy.wait()


def edges(band_maps):
    maps, wide, bins = band_maps.shape
    vmem = pl.BlockSpec(memory_space=pltpu.VMEM)
    return pl.pallas_call(
        edge_kernel,
        in_specs=[pl.BlockSpec(memory_space=pltpu.HBM)],
        out_specs=[vmem, vmem],
        out_shape=[
            jax.ShapeDtypeStruct((maps, 128), BF16),
            jax.ShapeDtypeStruct(band_maps.shape, BF16),
        ],
        scratch_shapes=[pltpu.SemaphoreType.DMA((2, 4))],
        compiler_params=params(),
        cost_estimate=pl.CostEstimate(flops=2 * maps * wide * 128 * 160, bytes_accessed=2**22, transcendentals=0),
        name="edges",
    )(band_maps)


def windows(planes, win_ref, rows):
    wide = len(planes)
    for mid in range(1, wide - 1):
        one = planes[mid - 1] + planes[mid] + planes[mid + 1]
        win_ref[0, mid, rows, :] = one
        if 2 <= mid < wide - 2:
            win_ref[1, mid, rows, :] = one + (planes[mid - 2] + planes[mid + 2])


def box_of(win_ref, wider, centre):
    h = jnp.where(wider, 1, 0)
    reach = jnp.where(wider, 2, 0)
    outer = jnp.where(wider, 1.0, 0.0)
    scale = jnp.where(wider, 1.0 / 25.0, 1.0 / 9.0)

    def box(at, size):
        acc = win_ref[h, centre, pl.ds(at, size), :]
        acc = acc + win_ref[h, centre + 1, pl.ds(at - 1, size), :]
        acc = acc + win_ref[h, centre - 1, pl.ds(at + 1, size), :]
        far = win_ref[h, centre + reach, pl.ds(at - 2, size), :]
        far = far + win_ref[h, centre - reach, pl.ds(at + 2, size), :]
        return (acc + far * outer) * scale

    return box


def inner_kernel(
    ids_ref, half_ref, band_ref, sums_ref, total_ref, first_win_ref, last_win_ref, plane_ref, turned_ref, win_ref, perm_ref
):
    maps, wide, bins = band_ref.shape
    strata = sums_ref.shape[0]
    r = lax.broadcasted_iota(jnp.int32, (8 * wide, 8 * wide), 0)
    c = lax.broadcasted_iota(jnp.int32, (8 * wide, 8 * wide), 1)
    perm_ref[...] = (c == lax.rem(r, 8) * wide + lax.div(r, 8)).astype(BF16)
    for g in range(maps // 8):
        group = jnp.dot(
            perm_ref[...], band_ref[pl.ds(8 * g, 8)].reshape(8 * wide, bins), preferred_element_type=F32
        )
        plane_ref[:, pl.ds(8 * g, 8), :] = group.reshape(wide, 8, bins)

    def turn(d, carry):
        for half in range(bins // 128):
            tile = plane_ref[d, :, half * 128 : half * 128 + 128]
            turned_ref[d, pl.ds(half * 128, 128), :] = jnp.transpose(tile)
        return carry

    lax.fori_loop(0, wide, turn, 0, unroll=4)

    def some(i, carry):
        rows = pl.ds(pl.multiple_of(i * 16, 16), 16)
        windows([turned_ref[d, rows, :] for d in range(wide)], win_ref, rows)
        return carry

    lax.fori_loop(0, bins // 16, some, 0)
    first_win_ref[...] = win_ref[:, :, pl.ds(0, 8), :]
    last_win_ref[...] = win_ref[:, :, pl.ds(bins - 8, 8), :]

    def stratum(k, carry):
        box = box_of(win_ref, half_ref[k] >= 2, ids_ref[k])
        total = jnp.zeros((1, maps), F32)
        for at in range(0, bins - TAIL, 64):
            size = min(64, bins - TAIL - at)
            part = box(at + 2, size)
            sums_ref[k, pl.ds(at, size), :] = part
            total = total + jnp.sum(part, axis=0, keepdims=True)
        total_ref[k] = jnp.broadcast_to(total, (8, maps))
        return carry

    lax.fori_loop(0, strata, stratum, 0, unroll=2)


def inner(band_maps, stratum_ids, half_width):
    maps, wide, bins = band_maps.shape
    strata = stratum_ids.shape[0]
    smem = pl.BlockSpec(memory_space=pltpu.SMEM)
    vmem = pl.BlockSpec(memory_space=pltpu.VMEM)
    return pl.pallas_call(
        inner_kernel,
        in_specs=[smem, smem, vmem],
        out_specs=[vmem, vmem, vmem, vmem],
        out_shape=[
            jax.ShapeDtypeStruct((strata, bins - TAIL, maps), F32),
            jax.ShapeDtypeStruct((strata, 8, maps), F32),
            jax.ShapeDtypeStruct((2, wide, 8, maps), F32),
            jax.ShapeDtypeStruct((2, wide, 8, maps), F32),
        ],
        scratch_shapes=[
            pltpu.VMEM((wide, maps, bins), F32),
            pltpu.VMEM((wide, bins, maps), F32),
            pltpu.VMEM((2, wide, bins, maps), F32),
            pltpu.VMEM((8 * wide, 8 * wide), BF16),
        ],
        compiler_params=params(),
        cost_estimate=pl.CostEstimate(flops=2 * maps * wide * bins * 256, bytes_accessed=2**22, transcendentals=0),
        name="inner",
    )(stratum_ids, half_width, band_maps)


def words_of(value):
    hi = value.astype(BF16).astype(F32)
    mid = (value - hi).astype(BF16).astype(F32)
    return hi, mid, value - hi - mid


def smooth_kernel(
    ids_ref, half_ref, sums_ref, total_ref, first_win_ref, last_win_ref, next_ref, out_ref, win_ref, start_ref
):
    strata, ready, maps = sums_ref.shape
    wide = first_win_ref.shape[1]
    bins = ready + TAIL
    y, z, x = (lax.axis_index(a) for a in BINS_AXES)
    last_y, last_z, last_x = (lax.axis_size(a) - 1 for a in BINS_AXES)
    before = (z == last_z) & (x == last_x)
    after = (z == 0) & (x == 0)
    ahead = jnp.where(before, 0.0, jnp.transpose(next_ref[...].astype(F32)))
    row8 = lax.broadcasted_iota(jnp.int32, (8, maps), 0)
    tails = []
    for d in range(wide):
        at = HALO * d
        tile = pltpu.roll(ahead[at // 8 * 8 : at // 8 * 8 + 8], (-(at % 8)) % 8, axis=0)
        tails.append(jnp.where(row8 < HALO, tile, 0.0))
    win_ref[:, :, pl.ds(0, 8), :] = last_win_ref[...]
    windows(tails, win_ref, pl.ds(8, 8))
    start_ref[:, :, pl.ds(0, 8), :] = jnp.zeros((2, wide, 8, maps), F32)
    start_ref[:, :, pl.ds(8, 8), :] = first_win_ref[...]

    row = lax.broadcasted_iota(jnp.int32, (16, maps), 0)
    empty = before & (row8 >= 8 - 2 * RIM)
    seam_before = before & (row8 < 2 * RIM) & ((y < last_y) | (row8 < RIM))
    seam_after = after & (row8 < 2 * RIM) & ((y > 0) | (row8 >= RIM))
    per_slot = jnp.where(before, 1.0 / (bins - 2 * RIM), 1.0 / bins)

    def stratum(k, carry):
        wider, centre = half_ref[k] >= 2, ids_ref[k]
        end = box_of(win_ref, wider, centre)(2, 8)
        total = total_ref[k][:1] + jnp.sum(jnp.where(empty, 0.0, end), axis=0, keepdims=True)
        mean = total * per_slot
        for at in range(0, bins, 64):
            size = min(64, ready - at)
            part = sums_ref[k, pl.ds(at, size), :]
            if size < 64:
                part = jnp.concatenate([part, jnp.where(empty, mean, end)], axis=0)
            out_ref[k, pl.ds(at, 64), :] = (part - mean).astype(BF16)
        seam = jnp.where(seam_before, pltpu.roll(end, 2 * RIM, axis=0), 0.0)
        seam = seam + jnp.where(seam_after, box_of(start_ref, wider, centre)(8 - RIM, 8), 0.0)
        side = jnp.zeros((16, maps), F32)
        for i, (m, v) in enumerate(zip(words_of(mean), words_of(seam))):
            v = jnp.concatenate([v, jnp.zeros((8, maps), F32)], axis=0)
            side = jnp.where(row == i, m, side) + pltpu.roll(v, 3 + 2 * RIM * i, axis=0)
        out_ref[k, pl.ds(bins, 16), :] = side.astype(BF16)
        return carry

    lax.fori_loop(0, strata, stratum, 0, unroll=2)


def smoothed(sums, total, first_win, last_win, ahead, stratum_ids, half_width):
    strata, ready, maps = sums.shape
    wide = first_win.shape[1]
    smem = pl.BlockSpec(memory_space=pltpu.SMEM)
    vmem = pl.BlockSpec(memory_space=pltpu.VMEM)
    return pl.pallas_call(
        smooth_kernel,
        in_specs=[smem, smem] + [vmem] * 5,
        out_specs=vmem,
        out_shape=jax.ShapeDtypeStruct((strata, ready + TAIL + 16, maps), BF16),
        scratch_shapes=[
            pltpu.VMEM((2, wide, 16, maps), F32),
            pltpu.VMEM((2, wide, 16, maps), F32),
        ],
        compiler_params=params(),
        name="smooth",
    )(stratum_ids, half_width, sums, total, first_win, last_win, ahead)


def dot_tn(a, b):
    return lax.dot_general(
        a, b, (((0,), (0,)), ((), ())), precision=lax.Precision.HIGHEST, preferred_element_type=F32
    )


def gram_kernel(blocks, panels, cores, sum_y, sum_x, bins, in_ref, out_ref, data_ref, mean_ref, gram_ref):
    maps = 128
    total = panels * maps
    seam = []
    for m in range(panels):
        parts = []
        for z in range(blocks):
            src = place(z, m, blocks, cores)
            data_ref[pl.ds(z * bins, bins), pl.ds(m * maps, maps)] = in_ref[src, pl.ds(0, bins), :]
            words = in_ref[src, pl.ds(bins, 16), :].astype(F32)
            mean_ref[z : z + 1, m * maps : (m + 1) * maps] = words[0:1] + words[1:2] + words[2:3]
            parts.append(words[3:7] + words[7:11] + words[11:15])
        seam.append(sum(parts))
    means = mean_ref[:blocks, :]
    short = lax.axis_index("x") == sum_x - 1
    z = lax.broadcasted_iota(jnp.int32, (blocks, 1), 0)
    count = jnp.where(short & (z == blocks - 1), float(bins - 2 * RIM), float(bins))
    centre = jnp.sum(means * count, axis=0, keepdims=True)
    centre = centre * jnp.where(short, 1.0 / (blocks * bins - 2 * RIM), 1.0 / (blocks * bins))
    dev = means - centre
    hi, mid, low = words_of(dev)
    left_hi, left_mid, left_low = words_of(dev * count)
    empty = jnp.zeros((32 - 6 * blocks, total), F32)
    left = jnp.concatenate([left_hi, left_hi, left_mid, left_mid, left_hi, left_low, empty], axis=0)
    right = jnp.concatenate([hi, mid, hi, mid, low, hi, empty], axis=0)
    tn = (((0,), (0,)), ((), ()))
    data = data_ref[...]
    gram_ref[...] = lax.dot_general(data, data, tn, preferred_element_type=F32) + lax.dot_general(
        left.astype(BF16), right.astype(BF16), tn, preferred_element_type=F32
    )
    r = lax.broadcasted_iota(jnp.int32, (maps, maps), 0)
    c = lax.broadcasted_iota(jnp.int32, (maps, maps), 1)
    side = [centre[:, m * maps : (m + 1) * maps] for m in range(panels)]
    for m in range(panels):
        block = gram_ref[pl.ds(m * maps, maps), pl.ds(m * maps, maps)]
        side.append(jnp.sum(jnp.where(r == c, block, 0.0), axis=0, keepdims=True))
    side = jnp.concatenate(side + seam, axis=0)
    per = maps // (blocks * sum_x)
    for y in range(sum_y):
        for x in range(sum_x):
            d = x * sum_y + y
            for m in range(panels):
                for z in range(blocks):
                    q = y * maps + (z * sum_x + x) * per
                    out_ref[d, pl.ds((m * blocks + z) * per, per), :] = gram_ref[
                        pl.ds(q, per), pl.ds(m * maps, maps)
                    ]
            out_ref[d, pl.ds(panels * blocks * per, SIDE * panels), :] = side


def partial_gram(received, blocks, panels, cores, sum_y, sum_x):
    bins = received.shape[1] - 16
    total = panels * 128
    per = 128 // (blocks * sum_x)
    vmem = pl.BlockSpec(memory_space=pltpu.VMEM)
    return pl.pallas_call(
        lambda *refs: gram_kernel(blocks, panels, cores, sum_y, sum_x, bins, *refs),
        in_specs=[vmem],
        out_specs=vmem,
        out_shape=jax.ShapeDtypeStruct(
            (sum_y * sum_x, panels * blocks * per + SIDE * panels, 128), F32
        ),
        scratch_shapes=[
            pltpu.VMEM((blocks * bins, total), BF16),
            pltpu.VMEM((8, total), F32),
            pltpu.VMEM((total, total), F32),
        ],
        compiler_params=params(),
        name="partial_gram",
    )(received)


def sum_kernel(blocks, panels, cores, sum_y, sum_x, count, in_ref, out_ref, mean_ref, between_ref, spread_ref):
    maps = 128
    parts = in_ref.shape[0]
    rows = in_ref.shape[1] - SIDE * panels
    per = rows // (panels * blocks)
    total_bins = float(count * parts)
    for m in range(panels):
        cols = slice(m * maps, (m + 1) * maps)
        mean_ref[:parts, cols] = jnp.concatenate(
            [in_ref[d, pl.ds(rows + m, 1), :] for d in range(parts)], axis=0
        )
        at = pl.ds(rows + 2 * panels + 2 * RIM * m, 2 * RIM)
        for y in range(sum_y):
            before = in_ref[(sum_x - 1) * sum_y + y, at, :]
            mean_ref[pl.ds(parts + 2 * RIM * y, 2 * RIM), cols] = before + in_ref[(y + 1) % sum_y, at, :]
    means = mean_ref[...]
    row = lax.broadcasted_iota(jnp.int32, (means.shape[0], 1), 0)
    weight = jnp.where(row < parts, float(count), 1.0)
    weight = jnp.where((row < parts) & (row >= parts - sum_y), float(count - 2 * RIM), weight)
    dev = means - jnp.sum(means * weight, axis=0, keepdims=True) * (1.0 / total_bins)
    own = jnp.concatenate(
        [
            sum(in_ref[d, pl.ds(rows + panels + m, 1), :] for d in range(parts))
            for m in range(panels)
        ],
        axis=1,
    )
    spread = (own + jnp.sum(dev * dev * weight, axis=0, keepdims=True)) * (1.0 / total_bins)
    y = lax.axis_index("y")
    x = lax.axis_index("x")
    for m in range(panels):

        @pl.when(y == m)
        def _():
            cols = slice(m * maps, (m + 1) * maps)
            between_ref[...] = dot_tn(dev[:, cols] * weight, dev)
            spread_ref[...] = jnp.transpose(jnp.broadcast_to(spread[:, cols], (maps, maps)))

    for z in range(blocks):
        start = pl.multiple_of((z * sum_x + x) * per, per)
        between = between_ref[pl.ds(start, per), :]
        spread_q = spread_ref[pl.ds(start, per), :]
        for m in range(panels):
            tile = pl.ds((m * blocks + z) * per, per)
            acc = in_ref[0, tile, :]
            for d in range(1, parts):
                acc = acc + in_ref[d, tile, :]
            cols = slice(m * maps, (m + 1) * maps)
            dest = place(z, m, blocks, cores)
            out_ref[dest, pl.ds(0, per), :] = (acc + between[:, cols]) * (1.0 / total_bins)
            out_ref[dest, pl.ds(per, per), :] = jnp.sqrt(spread_q * spread[:, cols])


def summed(received, blocks, panels, cores, sum_y, sum_x, count):
    parts = received.shape[0]
    per = (received.shape[1] - SIDE * panels) // (panels * blocks)
    vmem = pl.BlockSpec(memory_space=pltpu.VMEM)
    return pl.pallas_call(
        lambda *refs: sum_kernel(blocks, panels, cores, sum_y, sum_x, count, *refs),
        in_specs=[vmem],
        out_specs=vmem,
        out_shape=jax.ShapeDtypeStruct((blocks * panels, 2 * per, 128), F32),
        scratch_shapes=[
            pltpu.VMEM((parts + 2 * RIM * sum_y, panels * 128), F32),
            pltpu.VMEM((128, panels * 128), F32),
            pltpu.VMEM((128, 128), F32),
        ],
        compiler_params=params(),
        name="sum_parts",
    )(received)


def final_kernel(in_ref, gram_ref, scc_ref):
    strata, rows, _ = in_ref.shape
    per = rows // 2
    top = jnp.zeros((per, 128), F32)
    bottom = jnp.zeros((per, 128), F32)
    for k in range(strata):
        tile = in_ref[k, pl.ds(0, per), :]
        gram_ref[:, k, :] = tile
        top = top + tile
        bottom = bottom + in_ref[k, pl.ds(per, per), :]
    scc_ref[...] = top / bottom


def final(received):
    strata, rows, lanes = received.shape
    vmem = pl.BlockSpec(memory_space=pltpu.VMEM)
    return pl.pallas_call(
        final_kernel,
        in_specs=[vmem],
        out_specs=[vmem, vmem],
        out_shape=[
            jax.ShapeDtypeStruct((rows // 2, strata, lanes), F32),
            jax.ShapeDtypeStruct((rows // 2, lanes), F32),
        ],
        compiler_params=params(),
        name="final",
    )(received)


def body(band_maps, stratum_ids, half_width):
    maps, wide, bins = band_maps.shape
    blocks, sum_y, sum_x = (lax.axis_size(a) for a in ("zl", "y", "x"))
    panels = lax.axis_size(MAPS_AXES)
    cores = lax.axis_size("core")
    edge, band_maps = edges(pltpu.with_memory_space_constraint(band_maps, pltpu.HBM))
    ahead = lax.ppermute(edge, HALO_AXES, next_to_here())
    ready = inner(band_maps, stratum_ids, half_width)
    strata = smoothed(*ready, ahead, stratum_ids, half_width)
    strata = lax.all_to_all(strata, STRATA_AXES, 0, 0, tiled=True)
    parts = partial_gram(strata, blocks, panels, cores, sum_y, sum_x)
    parts = lax.all_to_all(parts, SUM_AXES, 0, 0, tiled=True)
    tiles = summed(parts, blocks, panels, cores, sum_y, sum_x, blocks * bins)
    tiles = lax.all_to_all(tiles, STRATA_AXES, 0, 0, tiled=True)
    gram, scc = final(tiles)
    return gram, scc


def solution(mesh):
    split = Mesh(mesh.devices.reshape(4, 4, 4, 2, 2), BINS_AXES + MAPS_AXES)
    in_specs = (P(MAPS_AXES, None, BINS_AXES), P(), P())
    out_specs = (P(BINS_AXES, None, MAPS_AXES), P(BINS_AXES, MAPS_AXES))
    return jax.shard_map(body, mesh=split, in_specs=in_specs, out_specs=out_specs, check_vma=False)
```

time: 103 us -> 90.7 us (0.88)
  blocking collectives: 84.2 us -> 71 us
  starting transfers between devices: 5.86 us -> 8.67 us
  local copies, waits for them, and re-layouts: 1.59 us -> 0.01 us
    all_to_all x1, blocking collectives: 45.7 us -> 34.1 us  [body(): strata = lax.all_to_all(strata, STRATA_AXES, 0, 0, tiled=True)]
    ppermute x2 -> x1, starting transfers between devices: 5.86 us -> 8.67 us  [body(): ahead = lax.ppermute(edge, HALO_AXES, next_to_here())]
    all_to_all x1, blocking collectives: 25.9 us -> 23.6 us  [body(): parts = lax.all_to_all(parts, SUM_AXES, 0, 0, tiled=True)]
    unnamed x6 -> x4, local copies, waits for them, and re-layouts: 1.59 us -> 0.01 us
    pallas_call x4 -> x5, Pallas kernels: 8.68 us -> 9.45 us  [the longest x1 4.26 us: inner(): pl.pallas_call(inner_kernel, in_specs=[smem, smem, vmem], out_specs=[vmem...]
  transfers between devices with their start and end apart: 2 -> 1, of which waited for: 1 -> 0; matrix products, arithmetic and copies ran while one was open for 0% -> 0% of each run, Pallas kernels for 0% -> 5%
where the time goes in v2:
time: 90.7 us; the launch traced here: 90.5 us
  blocking collectives  71 us (78%)
  Pallas kernels  10.1 us (11%)
  starting transfers between devices  8.67 us (10%)
    all_to_all x1, blocking collectives, body(): strata = lax.all_to_all(strata, STRATA_AXES, 0, 0, tiled=True)  34.1 us
    all_to_all x1, blocking collectives, body(): parts = lax.all_to_all(parts, SUM_AXES, 0, 0, tiled=True)  23.6 us
    all_to_all x1, blocking collectives, body(): tiles = lax.all_to_all(tiles, STRATA_AXES, 0, 0, tiled=True)  13.3 us
    ppermute x1, starting transfers between devices, body(): ahead = lax.ppermute(edge, HALO_AXES, next_to_here())  8.67 us
    pallas_call x1, Pallas kernels, inner(): pl.pallas_call(inner_kernel, in_specs=[smem, smem, vmem], out_specs=[vmem...  4.26 us
    pallas_call x1, Pallas kernels, edges(): pl.pallas_call(edge_kernel, in_specs=[pl.BlockSpec(memory_space=pltpu.HBM...  2.56 us
  transfers between devices with their start and end apart: 1, of which 0 were waited for; matrix products, arithmetic and copies ran while one was open for 0% of the time, Pallas kernels for 5%

profile of v2, /device:TPU:1, one launch (start us, length us, event | category | flops | bytes accessed | tf_op | source)
XLA Modules:
  0.0 90.5 jit_solution(5442900968878394395)
XLA Ops:
  0.6 0.0 copy-start.1
  0.6 0.0 copy-start
  0.6 2.6 %edges.1 = (bf16[128,128]{1,0:T(8,128)(2,1)S(1)}, bf16[128,32,256]{2,1,0:T(8,128)(2,1)S(1)}) custom-call(bf16[128,32,256]{2,1,0:T(8,128)(2,1)} %band_ref.1), custom_call_target="tpu_custom_call" | custom-call | flops 167772160 | bytes 4194304 | tf_op jit(solution)/shard_map/edges/pallas_call | solution.py:81
  3.2 8.7 %collective-permute-start = (bf16[128,128]{1,0:T(8,128)(2,1)S(1)}, bf16[128,128]{1,0:T(8,128)(2,1)S(1)}, u32[]{:S(2)}, u32[]{:S(2)}) collective-permute-start(bf16[128,128]{1,0:T(8,128)(2,1)S(1)} %get-tuple-element.13), channel_id=1, source_target_pairs={{4,0},{8,4},{12,8},{16,12},{20,16},{24,20},{28,24},{32,28},{36,32}... | collective-permute-start | bytes 98312 | tf_op jit(solution)/shard_map/ppermute | solution.py:455
  11.9 0.0 copy-done.1
  11.9 0.0 copy-done
  11.9 4.3 %inner.1 = (f32[16,248,128]{2,1,0:T(8,128)S(1)}, f32[16,8,128]{2,1,0:T(8,128)S(1)}, f32[2,32,8,128]{3,2,1,0:T(8,128)S(1)}, f32[2,32,8,128]{3,2,1,0:T(8,128)S(1)}) custom-call(s32[16]{0:T(128)S(1)} %copy-done, s32[16]{0:T(128)S(1)} %copy-done.1, bf16[128,32,256]{2,1,0:T(8,128)(2,1)S(1)} %get-tuple-element.8.band_ref), custom_call_target="tpu_custom_call" | custom-call | flops 536870912 | bytes 4194304 | tf_op jit(solution)/shard_map/inner/pallas_call | solution.py:172
  16.2 0.0 collective-permute-done.next_ref
  16.2 1.1 %smooth.1 = bf16[16,272,128]{2,1,0:T(8,128)(2,1)S(1)} custom-call(s32[16]{0:T(128)S(1)} %copy-done, s32[16]{0:T(128)S(1)} %copy-done.1, f32[16,248,128]{2,1,0:T(8,128)S(1)} %get-tuple-element.9.sums_ref, f32[16,8,128]{2,1,0:T(8,128)S(1)} %get-tuple-element.10.total_ref, f32[2,32,8,128]{3,2,1,0:T(8,128)S(1)} %get-tuple-element.11.first_win_ref, ...), custom_call_target="tpu_custom_call" | custom-call | tf_op jit(solution)/shard_map/smooth/pallas_call | solution.py:256
  17.3 34.1 %all_to_all.15.refs_0_ = bf16[16,272,128]{2,1,0:T(8,128)(2,1)S(1)} all-to-all(bf16[16,272,128]{2,1,0:T(8,128)(2,1)S(1)} %smooth.1), channel_id=1, replica_groups=mesh['y'=4,'zl'=4,'x'=4,'zh'=2,'core'=2] {'zh','zl','core'}, dimensions={0} | all-to-all | bytes 2228224 | tf_op jit(solution)/shard_map/all_to_all | solution.py:458
  51.4 1.0 %partial_gram.1 = f32[16,152,128]{2,1,0:T(8,128)S(1)} custom-call(bf16[16,272,128]{2,1,0:T(8,128)(2,1)S(1)} %all_to_all.15.refs_0_), custom_call_target="tpu_custom_call" | custom-call | tf_op jit(solution)/shard_map/partial_gram/pallas_call | solution.py:331
  52.4 23.6 %all_to_all.16.refs_0_ = f32[16,152,128]{2,1,0:T(8,128)S(1)} all-to-all(f32[16,152,128]{2,1,0:T(8,128)S(1)} %partial_gram.1), channel_id=1, replica_groups=mesh['y'=4,'zl'=4,'x'=4,'zh'=2,'core'=2] {'x','y'}, dimensions={0} | all-to-all | bytes 2490368 | tf_op jit(solution)/shard_map/all_to_all | solution.py:460
  76.0 0.5 sum_parts.1
  76.5 13.3 %all_to_all.17.in_ref = f32[16,16,128]{2,1,0:T(8,128)S(1)} all-to-all(f32[16,16,128]{2,1,0:T(8,128)S(1)} %sum_parts.1), channel_id=1, replica_groups=mesh['y'=4,'zl'=4,'x'=4,'zh'=2,'core'=2] {'zh','zl','core'}, dimensions={0} | all-to-all | bytes 262144 | tf_op jit(solution)/shard_map/all_to_all | solution.py:462
  89.8 0.7 final.1
Async XLA Ops:
  0.6 11.3 %copy-start.1 = (s32[16]{0:T(128)S(1)}, s32[16]{0:T(128)}, u32[]{:S(2)}) copy-start(s32[16]{0:T(128)} %half_ref.3) | copy-start | bytes 196
  0.6 11.3 %copy-start = (s32[16]{0:T(128)S(1)}, s32[16]{0:T(128)}, u32[]{:S(2)}) copy-start(s32[16]{0:T(128)} %ids_ref.3) | copy-start | bytes 196
  3.2 12.9 %collective-permute-start = (bf16[128,128]{1,0:T(8,128)(2,1)S(1)}, bf16[128,128]{1,0:T(8,128)(2,1)S(1)}, u32[]{:S(2)}, u32[]{:S(2)}) collective-permute-start(bf16[128,128]{1,0:T(8,128)(2,1)S(1)} %get-tuple-element.13), channel_id=1, source_target_pairs={{4,0},{8,4},{12,8},{16,12},{20,16},{24,20},{28,24},{32,28},{36,32}... | collective-permute-start | bytes 98312 | tf_op jit(solution)/shard_map/ppermute | solution.py:455

commit v3 on v2

v3 whole, which is shorter than its diff:
```python
import jax
import jax.numpy as jnp
from jax import lax
from jax.experimental import pallas as pl
from jax.experimental.pallas import tpu as pltpu
from jax.sharding import Mesh, PartitionSpec as P

HMAX = 2
X_AXES = ("xh", "xl")
BINS_AXES = ("y", "zl") + X_AXES
MAPS_AXES = ("zh", "core")
HALO_AXES = BINS_AXES + ("zh",)
STRATA_AXES = ("zh", "zl", "xl")
SUM_AXES = ("xh", "y")
F32 = jnp.float32
BF16 = jnp.bfloat16
HALO = 4
TAIL = 8
RIM = 2
SIDE = 64
SPAN = 200.0
VMEM_LIMIT = 28 * 1024 * 1024


def place(zh, zl, xl, blocks, pairs):
    return (zh * blocks + zl) * pairs + xl


def next_to_here():
    zl, x, zh = (lax.axis_size(a) for a in ("zl", X_AXES, "zh"))
    pairs = []
    for y in range(lax.axis_size("y")):
        flat = [((y * zl + p // x % zl) * x + p % x) * zh + p // (x * zl) for p in range(zh * zl * x)]
        pairs += [(flat[(p + 1) % len(flat)], flat[p]) for p in range(len(flat))]
    return pairs


def params():
    return pltpu.CompilerParams(vmem_limit_bytes=VMEM_LIMIT)


def edge_kernel(band_ref, edge_ref, copy_ref, sems):
    maps, wide, bins = band_ref.shape
    copies = [
        pltpu.make_async_copy(band_ref.at[:, :, lanes], copy_ref.at[:, :, lanes], sems.at[half])
        for half, lanes in enumerate((pl.ds(0, 128), pl.ds(128, bins - 128)))
    ]
    for copy in copies:
        copy.start()
    column = lax.broadcasted_iota(jnp.int32, (128, 128), 0)
    part = lax.rem(lax.broadcasted_iota(jnp.int32, (128, 128), 1), HALO)
    pick = (column == part).astype(BF16)
    offset = lax.broadcasted_iota(jnp.int32, (wide, 128), 0)
    lane = lax.broadcasted_iota(jnp.int32, (wide, 128), 1)
    own = (lax.div(lane, HALO) == offset)[None]
    copies[0].wait()
    data = copy_ref[:, :, pl.ds(0, 128)].reshape(maps * wide, 128)
    spread = jnp.dot(data, pick, preferred_element_type=F32).reshape(maps, wide, 128)
    edge_ref[...] = jnp.sum(jnp.where(own, spread, 0.0), axis=1).astype(BF16)
    copies[1].wait()


def edges(band_maps):
    maps, wide, bins = band_maps.shape
    vmem = pl.BlockSpec(memory_space=pltpu.VMEM)
    return pl.pallas_call(
        edge_kernel,
        in_specs=[pl.BlockSpec(memory_space=pltpu.HBM)],
        out_specs=[vmem, vmem],
        out_shape=[
            jax.ShapeDtypeStruct((maps, 128), BF16),
            jax.ShapeDtypeStruct(band_maps.shape, BF16),
        ],
        scratch_shapes=[pltpu.SemaphoreType.DMA((2,))],
        compiler_params=params(),
        cost_estimate=pl.CostEstimate(flops=2 * maps * wide * 128 * 128, bytes_accessed=2**22, transcendentals=0),
        name="edges",
    )(band_maps)


def windows(planes, win_ref, rows):
    wide = len(planes)
    for mid in range(1, wide - 1):
        one = planes[mid - 1] + planes[mid] + planes[mid + 1]
        win_ref[0, mid, rows, :] = one
        if 2 <= mid < wide - 2:
            win_ref[1, mid, rows, :] = one + (planes[mid - 2] + planes[mid + 2])


def box_of(win_ref, wider, centre):
    h = jnp.where(wider, 1, 0)
    reach = jnp.where(wider, 2, 0)
    outer = jnp.where(wider, 1.0, 0.0)
    scale = jnp.where(wider, 1.0 / 25.0, 1.0 / 9.0)

    def box(at, size):
        acc = win_ref[h, centre, pl.ds(at, size), :]
        acc = acc + win_ref[h, centre + 1, pl.ds(at - 1, size), :]
        acc = acc + win_ref[h, centre - 1, pl.ds(at + 1, size), :]
        far = win_ref[h, centre + reach, pl.ds(at - 2, size), :]
        far = far + win_ref[h, centre - reach, pl.ds(at + 2, size), :]
        return (acc + far * outer) * scale

    return box


def inner_kernel(
    ids_ref, half_ref, band_ref, sums_ref, total_ref, first_win_ref, last_win_ref, plane_ref, turned_ref, win_ref, perm_ref
):
    maps, wide, bins = band_ref.shape
    strata = sums_ref.shape[0]
    r = lax.broadcasted_iota(jnp.int32, (8 * wide, 8 * wide), 0)
    c = lax.broadcasted_iota(jnp.int32, (8 * wide, 8 * wide), 1)
    perm_ref[...] = (c == lax.rem(r, 8) * wide + lax.div(r, 8)).astype(BF16)
    for g in range(maps // 8):
        group = jnp.dot(
            perm_ref[...], band_ref[pl.ds(8 * g, 8)].reshape(8 * wide, bins), preferred_element_type=F32
        )
        plane_ref[:, pl.ds(8 * g, 8), :] = group.reshape(wide, 8, bins)

    def turn(d, carry):
        for half in range(bins // 128):
            tile = plane_ref[d, :, half * 128 : half * 128 + 128]
            turned_ref[d, pl.ds(half * 128, 128), :] = jnp.transpose(tile)
        return carry

    lax.fori_loop(0, wide, turn, 0, unroll=4)

    def some(i, carry):
        rows = pl.ds(pl.multiple_of(i * 16, 16), 16)
        windows([turned_ref[d, rows, :] for d in range(wide)], win_ref, rows)
        return carry

    lax.fori_loop(0, bins // 16, some, 0)
    first_win_ref[...] = win_ref[:, :, pl.ds(0, 8), :]
    last_win_ref[...] = win_ref[:, :, pl.ds(bins - 8, 8), :]

    def stratum(k, carry):
        box = box_of(win_ref, half_ref[k] >= 2, ids_ref[k])
        total = jnp.zeros((1, maps), F32)
        for at in range(0, bins - TAIL, 64):
            size = min(64, bins - TAIL - at)
            part = box(at + 2, size)
            sums_ref[k, pl.ds(at, size), :] = part
            total = total + jnp.sum(part, axis=0, keepdims=True)
        total_ref[k] = jnp.broadcast_to(total, (8, maps))
        return carry

    lax.fori_loop(0, strata, stratum, 0, unroll=2)


def inner(band_maps, stratum_ids, half_width):
    maps, wide, bins = band_maps.shape
    strata = stratum_ids.shape[0]
    smem = pl.BlockSpec(memory_space=pltpu.SMEM)
    vmem = pl.BlockSpec(memory_space=pltpu.VMEM)
    return pl.pallas_call(
        inner_kernel,
        in_specs=[smem, smem, vmem],
        out_specs=[vmem, vmem, vmem, vmem],
        out_shape=[
            jax.ShapeDtypeStruct((strata, bins - TAIL, maps), F32),
            jax.ShapeDtypeStruct((strata, 8, maps), F32),
            jax.ShapeDtypeStruct((2, wide, 8, maps), F32),
            jax.ShapeDtypeStruct((2, wide, 8, maps), F32),
        ],
        scratch_shapes=[
            pltpu.VMEM((wide, maps, bins), F32),
            pltpu.VMEM((wide, bins, maps), F32),
            pltpu.VMEM((2, wide, bins, maps), F32),
            pltpu.VMEM((8 * wide, 8 * wide), BF16),
        ],
        compiler_params=params(),
        cost_estimate=pl.CostEstimate(flops=2 * maps * wide * bins * 256, bytes_accessed=2**22, transcendentals=0),
        name="inner",
    )(stratum_ids, half_width, band_maps)


def words_of(value):
    hi = value.astype(BF16).astype(F32)
    mid = (value - hi).astype(BF16).astype(F32)
    return hi, mid, value - hi - mid


def smooth_kernel(
    ids_ref, half_ref, sums_ref, total_ref, first_win_ref, last_win_ref, next_ref, out_ref, win_ref, start_ref
):
    strata, ready, maps = sums_ref.shape
    wide = first_win_ref.shape[1]
    bins = ready + TAIL
    y, z, x = (lax.axis_index(a) for a in ("y", "zl", X_AXES))
    last_y, last_z, last_x = (lax.axis_size(a) - 1 for a in ("y", "zl", X_AXES))
    before = (z == last_z) & (x == last_x)
    after = (z == 0) & (x == 0)
    ahead = jnp.where(before, 0.0, jnp.transpose(next_ref[...].astype(F32)))
    row8 = lax.broadcasted_iota(jnp.int32, (8, maps), 0)
    tails = []
    for d in range(wide):
        at = HALO * d
        tile = pltpu.roll(ahead[at // 8 * 8 : at // 8 * 8 + 8], (-(at % 8)) % 8, axis=0)
        tails.append(jnp.where(row8 < HALO, tile, 0.0))
    win_ref[:, :, pl.ds(0, 8), :] = last_win_ref[...]
    windows(tails, win_ref, pl.ds(8, 8))
    start_ref[:, :, pl.ds(0, 8), :] = jnp.zeros((2, wide, 8, maps), F32)
    start_ref[:, :, pl.ds(8, 8), :] = first_win_ref[...]

    row = lax.broadcasted_iota(jnp.int32, (16, maps), 0)
    empty = before & (row8 >= 8 - 2 * RIM)
    seam_before = before & (row8 < 2 * RIM) & ((y < last_y) | (row8 < RIM))
    seam_after = after & (row8 < 2 * RIM) & ((y > 0) | (row8 >= RIM))
    per_slot = jnp.where(before, 1.0 / (bins - 2 * RIM), 1.0 / bins)

    def stratum(k, carry):
        wider, centre = half_ref[k] >= 2, ids_ref[k]
        end = box_of(win_ref, wider, centre)(2, 8)
        total = total_ref[k][:1] + jnp.sum(jnp.where(empty, 0.0, end), axis=0, keepdims=True)
        mean = total * per_slot
        square = jnp.zeros((1, maps), F32)
        for at in range(0, bins, 64):
            size = min(64, ready - at)
            part = sums_ref[k, pl.ds(at, size), :]
            if size < 64:
                part = jnp.concatenate([part, jnp.where(empty, mean, end)], axis=0)
            part = part - mean
            square = square + jnp.sum(part * part, axis=0, keepdims=True)
            out_ref[k, pl.ds(at, 64), :] = part.astype(BF16)
        seam = jnp.where(seam_before, pltpu.roll(end, 2 * RIM, axis=0), 0.0)
        seam = seam + jnp.where(seam_after, box_of(start_ref, wider, centre)(8 - RIM, 8), 0.0)
        side = jnp.zeros((16, maps), F32)
        for i, value in enumerate(words_of(mean) + words_of(square)):
            side = jnp.where(row == i, value, side)
        for i, value in enumerate(words_of(seam)[:2]):
            value = jnp.concatenate([value, jnp.zeros((8, maps), F32)], axis=0)
            side = side + pltpu.roll(value, 6 + 2 * RIM * i, axis=0)
        out_ref[k, pl.ds(bins, 16), :] = side.astype(BF16)
        return carry

    lax.fori_loop(0, strata, stratum, 0, unroll=2)


def smoothed(sums, total, first_win, last_win, ahead, stratum_ids, half_width):
    strata, ready, maps = sums.shape
    wide = first_win.shape[1]
    smem = pl.BlockSpec(memory_space=pltpu.SMEM)
    vmem = pl.BlockSpec(memory_space=pltpu.VMEM)
    return pl.pallas_call(
        smooth_kernel,
        in_specs=[smem, smem] + [vmem] * 5,
        out_specs=vmem,
        out_shape=jax.ShapeDtypeStruct((strata, ready + TAIL + 16, maps), BF16),
        scratch_shapes=[
            pltpu.VMEM((2, wide, 16, maps), F32),
            pltpu.VMEM((2, wide, 16, maps), F32),
        ],
        compiler_params=params(),
        name="smooth",
    )(stratum_ids, half_width, sums, total, first_win, last_win, ahead)


def encode(r):
    size = jnp.exp2(jnp.abs(r) * SPAN - 0.5 * SPAN)
    return jnp.where(r < 0.0, -size, size)


def decode(code):
    size = jnp.log2(jnp.abs(code)) * (1.0 / SPAN) + 0.5
    return jnp.where(code < 0.0, -size, size)


def dot_tn(a, b):
    return lax.dot_general(
        a, b, (((0,), (0,)), ((), ())), precision=lax.Precision.HIGHEST, preferred_element_type=F32
    )


def gram_kernel(blocks, halves, pairs, sum_y, sum_x, bins, own_ref, other_ref, out_ref, data_ref, mean_ref, gram_ref):
    maps = 128
    panels = 2 * halves
    total = panels * maps
    mine = halves * maps
    count_blocks = blocks * pairs
    squares, seams = [], []
    for m in range(panels):
        in_ref = (own_ref, other_ref)[m // halves]
        square, seam = [], []
        for z in range(blocks):
            for x in range(pairs):
                src = place(m % halves, z, x, blocks, pairs)
                b = z * pairs + x
                data_ref[pl.ds(b * bins, bins), pl.ds(m * maps, maps)] = in_ref[src, pl.ds(0, bins), :]
                words = in_ref[src, pl.ds(bins, 16), :].astype(F32)
                mean_ref[b : b + 1, m * maps : (m + 1) * maps] = words[0:1] + words[1:2] + words[2:3]
                square.append(words[3:4] + words[4:5] + words[5:6])
                seam.append(words[6:10] + words[10:14])
        squares.append(sum(square))
        seams.append(sum(seam))
    means = mean_ref[...]
    short = lax.axis_index("xh") == sum_x - 1
    b = lax.broadcasted_iota(jnp.int32, (count_blocks, 1), 0)
    count = jnp.where(short & (b == count_blocks - 1), float(bins - 2 * RIM), float(bins))
    centre = jnp.sum(means * count, axis=0, keepdims=True)
    centre = centre * jnp.where(short, 1.0 / (count_blocks * bins - 2 * RIM), 1.0 / (count_blocks * bins))
    dev = means - centre
    hi, mid, low = words_of(dev[:, :mine])
    left_hi, left_mid, left_low = words_of(dev * count)
    pad = -6 * count_blocks % 32
    left = [left_hi, left_hi, left_mid, left_mid, left_hi, left_low, jnp.zeros((pad, total), F32)]
    right = [hi, mid, hi, mid, low, hi, jnp.zeros((pad, mine), F32)]
    left, right = (jnp.concatenate(a, axis=0).astype(BF16) for a in (left, right))
    tn = (((0,), (0,)), ((), ()))
    gram_ref[...] = lax.dot_general(
        data_ref[...], data_ref[:, :mine], tn, preferred_element_type=F32
    ) + lax.dot_general(left, right, tn, preferred_element_type=F32)
    squares = jnp.concatenate(squares, axis=1) + jnp.sum(dev * dev * count, axis=0, keepdims=True)
    by_lane = jnp.where(squares > 0.0, lax.rsqrt(squares), 0.0)

    def rows_of(line):
        return jnp.concatenate([line[:, m * maps : (m + 1) * maps] for m in range(panels)], axis=0)

    side = words_of(rows_of(centre)) + words_of(rows_of(squares)) + words_of(jnp.concatenate(seams, axis=0))[:2]
    side += (jnp.zeros((SIDE - (6 + 4 * RIM) * panels, maps), F32),)
    side = jnp.concatenate(side, axis=0).astype(BF16)
    core = lax.axis_index("core")
    per = maps // (blocks * sum_x)
    for q in range(panels):
        y = (q % halves) * 2 + (core if q < halves else 1 - core)
        by_row = jnp.transpose(jnp.broadcast_to(by_lane[:, q * maps : (q + 1) * maps], (maps, maps)))
        for m in range(halves):
            cols = slice(m * maps, (m + 1) * maps)
            code = encode(gram_ref[pl.ds(q * maps, maps), cols] * by_row * by_lane[:, cols]).astype(BF16)
            for x in range(sum_x):
                for z in range(blocks):
                    at = (z * sum_x + x) * per
                    out_ref[x * sum_y + y, pl.ds((m * blocks + z) * per, per), :] = code[at : at + per]
    for d in range(sum_x * sum_y):
        out_ref[d, pl.ds(halves * blocks * per, SIDE), :] = side


def partial_gram(own, other, blocks, halves, pairs, sum_y, sum_x):
    bins = own.shape[1] - 16
    total = 2 * halves * 128
    per = 128 // (blocks * sum_x)
    vmem = pl.BlockSpec(memory_space=pltpu.VMEM)
    return pl.pallas_call(
        lambda *refs: gram_kernel(blocks, halves, pairs, sum_y, sum_x, bins, *refs),
        in_specs=[vmem, vmem],
        out_specs=vmem,
        out_shape=jax.ShapeDtypeStruct((sum_y * sum_x, halves * blocks * per + SIDE, 128), BF16),
        scratch_shapes=[
            pltpu.VMEM((blocks * pairs * bins, total), BF16),
            pltpu.VMEM((blocks * pairs, total), F32),
            pltpu.VMEM((total, total // 2), F32),
        ],
        compiler_params=params(),
        name="partial_gram",
    )(own, other)


def sum_kernel(
    blocks, halves, pairs, sum_y, sum_x, count, in_ref, out_ref, mean_ref, scale_ref, between_ref, spread_ref, column_ref
):
    maps = 128
    panels = 2 * halves
    parts = in_ref.shape[0]
    rows = in_ref.shape[1] - SIDE
    per = rows // (halves * blocks)
    tile = per // pairs
    total_bins = float(count * parts)
    squares = jnp.zeros((panels, maps), F32)
    seams = []
    for d in range(parts):
        side = in_ref[d, pl.ds(rows, SIDE), :].astype(F32)
        mean, square = (
            side[i : i + panels] + side[i + panels : i + 2 * panels] + side[i + 2 * panels : i + 3 * panels]
            for i in (0, 3 * panels)
        )
        size = 2 * RIM * panels
        seams.append(side[6 * panels : 6 * panels + size] + side[6 * panels + size : 6 * panels + 2 * size])
        squares = squares + square
        scale = jnp.sqrt(square)
        for m in range(panels):
            mean_ref[d : d + 1, m * maps : (m + 1) * maps] = mean[m : m + 1]
            scale_ref[d : d + 1, m * maps : (m + 1) * maps] = scale[m : m + 1]
    for y in range(sum_y):
        seam = seams[(sum_x - 1) * sum_y + y] + seams[(y + 1) % sum_y]
        for m in range(panels):
            mean_ref[pl.ds(parts + 2 * RIM * y, 2 * RIM), m * maps : (m + 1) * maps] = seam[
                2 * RIM * m : 2 * RIM * (m + 1)
            ]
    means = mean_ref[...]
    row = lax.broadcasted_iota(jnp.int32, (means.shape[0], 1), 0)
    weight = jnp.where(row < parts, float(count), 1.0)
    weight = jnp.where((row < parts) & (row >= parts - sum_y), float(count - 2 * RIM), weight)
    dev = means - jnp.sum(means * weight, axis=0, keepdims=True) * (1.0 / total_bins)
    own = jnp.concatenate([squares[m : m + 1] for m in range(panels)], axis=1)
    spread = (own + jnp.sum(dev * dev * weight, axis=0, keepdims=True)) * (1.0 / total_bins)
    scales = scale_ref[...]
    y = lax.axis_index("y")
    x = lax.axis_index("xh")
    rows_panel = y // 2 + jnp.where(y % 2 == lax.axis_index("core"), 0, halves)
    for m in range(panels):

        @pl.when(rows_panel == m)
        def _():
            cols = slice(m * maps, (m + 1) * maps)
            between_ref[...] = dot_tn(dev[:, cols] * weight, dev[:, : halves * maps])
            spread_ref[...] = jnp.transpose(jnp.broadcast_to(spread[:, cols], (maps, maps)))
            column = jnp.concatenate([scales[:, cols], jnp.zeros((maps - parts, maps), F32)], axis=0)
            column_ref[...] = jnp.transpose(column)

    for z in range(blocks):
        spot = pl.ds(pl.multiple_of((z * sum_x + x) * per, per), per)
        column = column_ref[spot, :]
        acc = [between_ref[spot, m * maps : (m + 1) * maps] for m in range(halves)]
        for d in range(parts):
            by_row = jnp.broadcast_to(column[:, d : d + 1], (per, maps))
            for m in range(halves):
                code = in_ref[d, pl.ds((m * blocks + z) * per, per), :].astype(F32)
                by_lane = scales[d : d + 1, m * maps : (m + 1) * maps]
                acc[m] = acc[m] + decode(code) * by_row * by_lane
        for m in range(halves):
            bottom = jnp.sqrt(spread_ref[spot, :] * spread[:, m * maps : (m + 1) * maps])
            for j in range(pairs):
                dest = place(m, z, j, blocks, pairs)
                part = slice(j * tile, (j + 1) * tile)
                out_ref[dest, pl.ds(0, tile), :] = acc[m][part] * (1.0 / total_bins)
                out_ref[dest, pl.ds(tile, tile), :] = bottom[part]


def summed(received, blocks, halves, pairs, sum_y, sum_x, count):
    parts = received.shape[0]
    tile = (received.shape[1] - SIDE) // (halves * blocks * pairs)
    total = 2 * halves * 128
    vmem = pl.BlockSpec(memory_space=pltpu.VMEM)
    return pl.pallas_call(
        lambda *refs: sum_kernel(blocks, halves, pairs, sum_y, sum_x, count, *refs),
        in_specs=[vmem],
        out_specs=vmem,
        out_shape=jax.ShapeDtypeStruct((halves * blocks * pairs, 2 * tile, 128), F32),
        scratch_shapes=[
            pltpu.VMEM((parts + 2 * RIM * sum_y, total), F32),
            pltpu.VMEM((parts, total), F32),
            pltpu.VMEM((128, total // 2), F32),
            pltpu.VMEM((128, 128), F32),
            pltpu.VMEM((128, 128), F32),
        ],
        compiler_params=params(),
        name="sum_parts",
    )(received)


def final_kernel(in_ref, gram_ref, scc_ref):
    strata, rows, _ = in_ref.shape
    per = rows // 2
    top = jnp.zeros((per, 128), F32)
    bottom = jnp.zeros((per, 128), F32)
    for k in range(strata):
        tile = in_ref[k, pl.ds(0, per), :]
        gram_ref[:, k, :] = tile
        top = top + tile
        bottom = bottom + in_ref[k, pl.ds(per, per), :]
    scc_ref[...] = top / bottom


def final(received):
    strata, rows, lanes = received.shape
    vmem = pl.BlockSpec(memory_space=pltpu.VMEM)
    return pl.pallas_call(
        final_kernel,
        in_specs=[vmem],
        out_specs=[vmem, vmem],
        out_shape=[
            jax.ShapeDtypeStruct((rows // 2, strata, lanes), F32),
            jax.ShapeDtypeStruct((rows // 2, lanes), F32),
        ],
        compiler_params=params(),
        name="final",
    )(received)


def body(band_maps, stratum_ids, half_width):
    maps, wide, bins = band_maps.shape
    blocks, halves, pairs, sum_y, sum_x = (lax.axis_size(a) for a in ("zl", "zh", "xl", "y", "xh"))
    edge, band_maps = edges(pltpu.with_memory_space_constraint(band_maps, pltpu.HBM))
    ahead = lax.ppermute(edge, HALO_AXES, next_to_here())
    ready = inner(band_maps, stratum_ids, half_width)
    strata = smoothed(*ready, ahead, stratum_ids, half_width)
    strata = lax.all_to_all(strata, STRATA_AXES, 0, 0, tiled=True)
    other = lax.ppermute(strata, "core", [(0, 1), (1, 0)])
    parts = partial_gram(strata, other, blocks, halves, pairs, sum_y, sum_x)
    parts = lax.all_to_all(parts, SUM_AXES, 0, 0, tiled=True)
    tiles = summed(parts, blocks, halves, pairs, sum_y, sum_x, blocks * pairs * bins)
    tiles = lax.all_to_all(tiles, STRATA_AXES, 0, 0, tiled=True)
    gram, scc = final(tiles)
    return gram, scc


def solution(mesh):
    split = Mesh(mesh.devices.reshape(4, 4, 2, 2, 2, 2), BINS_AXES + MAPS_AXES)
    in_specs = (P(MAPS_AXES, None, BINS_AXES), P(), P())
    out_specs = (P(BINS_AXES, None, MAPS_AXES), P(BINS_AXES, MAPS_AXES))
    return jax.shard_map(body, mesh=split, in_specs=in_specs, out_specs=out_specs, check_vma=False)
```

time: 90.7 us -> 82.2 us (0.906)
  blocking collectives: 71 us -> 58 us
  waiting for transfers between devices: 0.01 us -> 2.38 us
  starting transfers between devices: 8.67 us -> 10.9 us
    all_to_all x1, blocking collectives: 23.6 us -> 14.5 us  [body(): parts = lax.all_to_all(parts, SUM_AXES, 0, 0, tiled=True)]
    ppermute x0 -> x1, waiting for transfers between devices: none -> 2.38 us  [body(): other = lax.ppermute(strata, 'core', [(0, 1), (1, 0)])]
    ppermute x0 -> x1, starting transfers between devices: none -> 2.2 us  [body(): other = lax.ppermute(strata, 'core', [(0, 1), (1, 0)])]
    all_to_all x1, blocking collectives: 13.3 us -> 11.1 us  [body(): tiles = lax.all_to_all(tiles, STRATA_AXES, 0, 0, tiled=True)]
    all_to_all x1, blocking collectives: 34.1 us -> 32.4 us  [body(): strata = lax.all_to_all(strata, STRATA_AXES, 0, 0, tiled=True)]
  transfers between devices with their start and end apart: 1 -> 2, of which waited for: 0 -> 1; matrix products, arithmetic and copies ran while one was open for 0% -> 0% of each run, Pallas kernels for 5% -> 5%
where the time goes in v3:
time: 82.2 us; the launch traced here: 81.4 us
  blocking collectives  58 us (71%)
  starting transfers between devices  10.9 us (13%)
  Pallas kernels  9.46 us (12%)
  waiting for transfers between devices  2.38 us (3%)
    all_to_all x1, blocking collectives, body(): strata = lax.all_to_all(strata, STRATA_AXES, 0, 0, tiled=True)  32.4 us
    all_to_all x1, blocking collectives, body(): parts = lax.all_to_all(parts, SUM_AXES, 0, 0, tiled=True)  14.5 us
    all_to_all x1, blocking collectives, body(): tiles = lax.all_to_all(tiles, STRATA_AXES, 0, 0, tiled=True)  11.1 us
    ppermute x1, starting transfers between devices, body(): ahead = lax.ppermute(edge, HALO_AXES, next_to_here())  8.68 us
    pallas_call x1, Pallas kernels, inner(): pl.pallas_call(inner_kernel, in_specs=[smem, smem, vmem], out_specs=[vmem...  4.26 us
    ppermute x1, waiting for transfers between devices, body(): other = lax.ppermute(strata, 'core', [(0, 1), (1, 0)])  2.38 us
    ppermute x1, starting transfers between devices, body(): other = lax.ppermute(strata, 'core', [(0, 1), (1, 0)])  2.2 us
    pallas_call x1, Pallas kernels, edges(): pl.pallas_call(edge_kernel, in_specs=[pl.BlockSpec(memory_space=pltpu.HBM...  1.67 us
  transfers between devices with their start and end apart: 2, of which 1 were waited for; matrix products, arithmetic and copies ran while one was open for 0% of the time, Pallas kernels for 5%

profile of v3, /device:TPU:1, one launch (start us, length us, event | category | flops | bytes accessed | tf_op | source)
XLA Modules:
  0.0 81.4 jit_solution(4734517897382478943)
XLA Ops:
  0.6 0.0 copy-start.1
  0.6 0.0 copy-start
  0.6 1.7 %edges.1 = (bf16[128,128]{1,0:T(8,128)(2,1)S(1)}, bf16[128,32,256]{2,1,0:T(8,128)(2,1)S(1)}) custom-call(bf16[128,32,256]{2,1,0:T(8,128)(2,1)} %band_ref.1), custom_call_target="tpu_custom_call" | custom-call | flops 134217728 | bytes 4194304 | tf_op jit(solution)/shard_map/edges/pallas_call | solution.py:66
  2.3 8.7 %collective-permute-start = (bf16[128,128]{1,0:T(8,128)(2,1)S(1)}, bf16[128,128]{1,0:T(8,128)(2,1)S(1)}, u32[]{:S(2)}, u32[]{:S(2)}) collective-permute-start(bf16[128,128]{1,0:T(8,128)(2,1)S(1)} %get-tuple-element.13), channel_id=1, source_target_pairs={{4,0},{8,4},{12,8},{16,12},{20,16},{24,20},{28,24},{32,28},{36,32}... | collective-permute-start | bytes 98312 | tf_op jit(solution)/shard_map/ppermute | solution.py:485
  11.0 0.0 copy-done.1
  11.0 0.0 copy-done
  11.0 4.3 %inner.1 = (f32[16,248,128]{2,1,0:T(8,128)S(1)}, f32[16,8,128]{2,1,0:T(8,128)S(1)}, f32[2,32,8,128]{3,2,1,0:T(8,128)S(1)}, f32[2,32,8,128]{3,2,1,0:T(8,128)S(1)}) custom-call(s32[16]{0:T(128)S(1)} %copy-done, s32[16]{0:T(128)S(1)} %copy-done.1, bf16[128,32,256]{2,1,0:T(8,128)(2,1)S(1)} %get-tuple-element.8.band_ref), custom_call_target="tpu_custom_call" | custom-call | flops 536870912 | bytes 4194304 | tf_op jit(solution)/shard_map/inner/pallas_call | solution.py:157
  15.3 0.0 collective-permute-done.next_ref
  15.3 1.3 %smooth.1 = bf16[16,272,128]{2,1,0:T(8,128)(2,1)S(1)} custom-call(s32[16]{0:T(128)S(1)} %copy-done, s32[16]{0:T(128)S(1)} %copy-done.1, f32[16,248,128]{2,1,0:T(8,128)S(1)} %get-tuple-element.9.sums_ref, f32[16,8,128]{2,1,0:T(8,128)S(1)} %get-tuple-element.10.total_ref, f32[2,32,8,128]{3,2,1,0:T(8,128)S(1)} %get-tuple-element.11.first_win_ref, ...), custom_call_target="tpu_custom_call" | custom-call | tf_op jit(solution)/shard_map/smooth/pallas_call | solution.py:246
  16.6 32.4 %all_to_all.15.refs_0_ = bf16[16,272,128]{2,1,0:T(8,128)(2,1)S(1)} all-to-all(bf16[16,272,128]{2,1,0:T(8,128)(2,1)S(1)} %smooth.1), channel_id=1, replica_groups=mesh['y'=4,'zl'=4,'xh'=2,'xl'=2,'zh'=2,'core'=2] {'zh','zl','xl'}, dimensions={0} | all-to-all | bytes 2228224 | tf_op jit(solution)/shard_map/all_to_all | solution.py:488
  49.0 2.2 %collective-permute-start.1 = (bf16[16,272,128]{2,1,0:T(8,128)(2,1)S(1)}, bf16[16,272,128]{2,1,0:T(8,128)(2,1)S(1)}, u32[]{:S(2)}, u32[]{:S(2)}) collective-permute-start(bf16[16,272,128]{2,1,0:T(8,128)(2,1)S(1)} %all_to_all.15.refs_0_), channel_id=1, source_target_pairs={{0,1},{1,0},{2,3},{3,2},{4,5},{5,4},{6,7},{7,6},{8,9},{9,8},{10,11... | collective-permute-start | bytes 3342344 | tf_op jit(solution)/shard_map/ppermute | solution.py:489
  51.2 2.4 %collective-permute-done.1.refs_1_ = bf16[16,272,128]{2,1,0:T(8,128)(2,1)S(1)} collective-permute-done((bf16[16,272,128]{2,1,0:T(8,128)(2,1)S(1)}, bf16[16,272,128]{2,1,0:T(8,128)(2,1)S(1)}, u32[]{:S(2)}, u32[]{:S(2)}) %collective-permute-start.1) | collective-permute-done | bytes 1114144 | tf_op jit(solution)/shard_map/ppermute | solution.py:489
  53.5 0.9 %partial_gram.1 = bf16[8,192,128]{2,1,0:T(8,128)(2,1)S(1)} custom-call(bf16[16,272,128]{2,1,0:T(8,128)(2,1)S(1)} %all_to_all.15.refs_0_, bf16[16,272,128]{2,1,0:T(8,128)(2,1)S(1)} %collective-permute-done.1.refs_1_), custom_call_target="tpu_custom_call" | custom-call | tf_op jit(solution)/shard_map/partial_gram/pallas_call | solution.py:344
  54.5 14.5 %all_to_all.16.refs_0_ = bf16[8,192,128]{2,1,0:T(8,128)(2,1)S(1)} all-to-all(bf16[8,192,128]{2,1,0:T(8,128)(2,1)S(1)} %partial_gram.1), channel_id=1, replica_groups=mesh['y'=4,'zl'=4,'xh'=2,'xl'=2,'zh'=2,'core'=2] {'xh','y'}, dimensions={0} | all-to-all | bytes 786432 | tf_op jit(solution)/shard_map/all_to_all | solution.py:491
  68.9 0.6 sum_parts.1
  69.6 11.1 %all_to_all.17.in_ref = f32[16,16,128]{2,1,0:T(8,128)S(1)} all-to-all(f32[16,16,128]{2,1,0:T(8,128)S(1)} %sum_parts.1), channel_id=1, replica_groups=mesh['y'=4,'zl'=4,'xh'=2,'xl'=2,'zh'=2,'core'=2] {'zh','zl','xl'}, dimensions={0} | all-to-all | bytes 262144 | tf_op jit(solution)/shard_map/all_to_all | solution.py:493
  80.7 0.7 final.1
Async XLA Ops:
  0.6 10.4 %copy-start.1 = (s32[16]{0:T(128)S(1)}, s32[16]{0:T(128)}, u32[]{:S(2)}) copy-start(s32[16]{0:T(128)} %half_ref.3) | copy-start | bytes 196
  0.6 10.4 %copy-start = (s32[16]{0:T(128)S(1)}, s32[16]{0:T(128)}, u32[]{:S(2)}) copy-start(s32[16]{0:T(128)} %ids_ref.3) | copy-start | bytes 196
  2.3 12.9 %collective-permute-start = (bf16[128,128]{1,0:T(8,128)(2,1)S(1)}, bf16[128,128]{1,0:T(8,128)(2,1)S(1)}, u32[]{:S(2)}, u32[]{:S(2)}) collective-permute-start(bf16[128,128]{1,0:T(8,128)(2,1)S(1)} %get-tuple-element.13), channel_id=1, source_target_pairs={{4,0},{8,4},{12,8},{16,12},{20,16},{24,20},{28,24},{32,28},{36,32}... | collective-permute-start | bytes 98312 | tf_op jit(solution)/shard_map/ppermute | solution.py:485
  49.0 4.6 %collective-permute-start.1 = (bf16[16,272,128]{2,1,0:T(8,128)(2,1)S(1)}, bf16[16,272,128]{2,1,0:T(8,128)(2,1)S(1)}, u32[]{:S(2)}, u32[]{:S(2)}) collective-permute-start(bf16[16,272,128]{2,1,0:T(8,128)(2,1)S(1)} %all_to_all.15.refs_0_), channel_id=1, source_target_pairs={{0,1},{1,0},{2,3},{3,2},{4,5},{5,4},{6,7},{7,6},{8,9},{9,8},{10,11... | collective-permute-start | bytes 3342344 | tf_op jit(solution)/shard_map/ppermute | solution.py:489

commit v4 on v3

--- a/solution.py
+++ b/solution.py
@@ -15,7 +15,7 @@
 F32 = jnp.float32
 BF16 = jnp.bfloat16
 HALO = 4
-TAIL = 8
+HEAD = 8
 RIM = 2
 SIDE = 64
 SPAN = 200.0
@@ -26,12 +26,12 @@
     return (zh * blocks + zl) * pairs + xl
 
 
-def next_to_here():
+def to_next():
     zl, x, zh = (lax.axis_size(a) for a in ("zl", X_AXES, "zh"))
     pairs = []
     for y in range(lax.axis_size("y")):
         flat = [((y * zl + p // x % zl) * x + p % x) * zh + p // (x * zl) for p in range(zh * zl * x)]
-        pairs += [(flat[(p + 1) % len(flat)], flat[p]) for p in range(len(flat))]
+        pairs += [(flat[p], flat[(p + 1) % len(flat)]) for p in range(len(flat))]
     return pairs
 
 
@@ -43,18 +43,18 @@
     maps, wide, bins = band_ref.shape
     copies = [
         pltpu.make_async_copy(band_ref.at[:, :, lanes], copy_ref.at[:, :, lanes], sems.at[half])
-        for half, lanes in enumerate((pl.ds(0, 128), pl.ds(128, bins - 128)))
+        for half, lanes in enumerate((pl.ds(bins - 128, 128), pl.ds(0, bins - 128)))
     ]
     for copy in copies:
         copy.start()
     column = lax.broadcasted_iota(jnp.int32, (128, 128), 0)
     part = lax.rem(lax.broadcasted_iota(jnp.int32, (128, 128), 1), HALO)
-    pick = (column == part).astype(BF16)
+    pick = (column == 128 - HALO + part).astype(BF16)
     offset = lax.broadcasted_iota(jnp.int32, (wide, 128), 0)
     lane = lax.broadcasted_iota(jnp.int32, (wide, 128), 1)
     own = (lax.div(lane, HALO) == offset)[None]
     copies[0].wait()
-    data = copy_ref[:, :, pl.ds(0, 128)].reshape(maps * wide, 128)
+    data = copy_ref[:, :, pl.ds(bins - 128, 128)].reshape(maps * wide, 128)
     spread = jnp.dot(data, pick, preferred_element_type=F32).reshape(maps, wide, 128)
     edge_ref[...] = jnp.sum(jnp.where(own, spread, 0.0), axis=1).astype(BF16)
     copies[1].wait()
@@ -112,19 +112,19 @@
     r = lax.broadcasted_iota(jnp.int32, (8 * wide, 8 * wide), 0)
     c = lax.broadcasted_iota(jnp.int32, (8 * wide, 8 * wide), 1)
     perm_ref[...] = (c == lax.rem(r, 8) * wide + lax.div(r, 8)).astype(BF16)
-    for g in range(maps // 8):
-        group = jnp.dot(
-            perm_ref[...], band_ref[pl.ds(8 * g, 8)].reshape(8 * wide, bins), preferred_element_type=F32
-        )
-        plane_ref[:, pl.ds(8 * g, 8), :] = group.reshape(wide, 8, bins)
-
-    def turn(d, carry):
+    for g in range(0, maps, 16):
+        pair = [
+            jnp.dot(
+                perm_ref[...], band_ref[pl.ds(g + 8 * j, 8)].reshape(8 * wide, bins), preferred_element_type=F32
+            ).reshape(wide, 8, bins)
+            for j in range(2)
+        ]
+        plane_ref[:, pl.ds(g, 16), :] = jnp.concatenate(pair, axis=1).astype(BF16)
+
+    for d in range(wide):
         for half in range(bins // 128):
             tile = plane_ref[d, :, half * 128 : half * 128 + 128]
-            turned_ref[d, pl.ds(half * 128, 128), :] = jnp.transpose(tile)
-        return carry
-
-    lax.fori_loop(0, wide, turn, 0, unroll=4)
+            turned_ref[d, pl.ds(half * 128, 128), :] = jnp.transpose(tile).astype(F32)
 
     def some(i, carry):
         rows = pl.ds(pl.multiple_of(i * 16, 16), 16)
@@ -138,15 +138,15 @@
     def stratum(k, carry):
         box = box_of(win_ref, half_ref[k] >= 2, ids_ref[k])
         total = jnp.zeros((1, maps), F32)
-        for at in range(0, bins - TAIL, 64):
-            size = min(64, bins - TAIL - at)
-            part = box(at + 2, size)
+        for at in range(0, bins - HEAD, 64):
+            size = min(64, bins - HEAD - at)
+            part = box(at + HEAD - RIM, size)
             sums_ref[k, pl.ds(at, size), :] = part
             total = total + jnp.sum(part, axis=0, keepdims=True)
         total_ref[k] = jnp.broadcast_to(total, (8, maps))
         return carry
 
-    lax.fori_loop(0, strata, stratum, 0, unroll=2)
+    lax.fori_loop(0, strata, stratum, 0, unroll=4)
 
 
 def inner(band_maps, stratum_ids, half_width):
@@ -159,13 +159,13 @@
         in_specs=[smem, smem, vmem],
         out_specs=[vmem, vmem, vmem, vmem],
         out_shape=[
-            jax.ShapeDtypeStruct((strata, bins - TAIL, maps), F32),
+            jax.ShapeDtypeStruct((strata, bins - HEAD, maps), F32),
             jax.ShapeDtypeStruct((strata, 8, maps), F32),
             jax.ShapeDtypeStruct((2, wide, 8, maps), F32),
             jax.ShapeDtypeStruct((2, wide, 8, maps), F32),
         ],
         scratch_shapes=[
-            pltpu.VMEM((wide, maps, bins), F32),
+            pltpu.VMEM((wide, maps, bins), BF16),
             pltpu.VMEM((wide, bins, maps), F32),
             pltpu.VMEM((2, wide, bins, maps), F32),
             pltpu.VMEM((8 * wide, 8 * wide), BF16),
@@ -183,49 +183,50 @@
 
 
 def smooth_kernel(
-    ids_ref, half_ref, sums_ref, total_ref, first_win_ref, last_win_ref, next_ref, out_ref, win_ref, start_ref
+    ids_ref, half_ref, sums_ref, total_ref, first_win_ref, last_win_ref, behind_ref, out_ref, start_ref, stop_ref
 ):
     strata, ready, maps = sums_ref.shape
     wide = first_win_ref.shape[1]
-    bins = ready + TAIL
+    bins = ready + HEAD
     y, z, x = (lax.axis_index(a) for a in ("y", "zl", X_AXES))
     last_y, last_z, last_x = (lax.axis_size(a) - 1 for a in ("y", "zl", X_AXES))
     before = (z == last_z) & (x == last_x)
     after = (z == 0) & (x == 0)
-    ahead = jnp.where(before, 0.0, jnp.transpose(next_ref[...].astype(F32)))
+    behind = jnp.where(after, 0.0, jnp.transpose(behind_ref[...].astype(F32)))
     row8 = lax.broadcasted_iota(jnp.int32, (8, maps), 0)
-    tails = []
+    heads = []
     for d in range(wide):
         at = HALO * d
-        tile = pltpu.roll(ahead[at // 8 * 8 : at // 8 * 8 + 8], (-(at % 8)) % 8, axis=0)
-        tails.append(jnp.where(row8 < HALO, tile, 0.0))
-    win_ref[:, :, pl.ds(0, 8), :] = last_win_ref[...]
-    windows(tails, win_ref, pl.ds(8, 8))
-    start_ref[:, :, pl.ds(0, 8), :] = jnp.zeros((2, wide, 8, maps), F32)
+        tile = pltpu.roll(behind[at // 8 * 8 : at // 8 * 8 + 8], (8 - HALO - at % 8) % 8, axis=0)
+        heads.append(jnp.where(row8 >= 8 - HALO, tile, 0.0))
+    windows(heads, start_ref, pl.ds(0, 8))
     start_ref[:, :, pl.ds(8, 8), :] = first_win_ref[...]
+    stop_ref[:, :, pl.ds(0, 8), :] = last_win_ref[...]
+    stop_ref[:, :, pl.ds(8, 8), :] = jnp.zeros((2, wide, 8, maps), F32)
 
     row = lax.broadcasted_iota(jnp.int32, (16, maps), 0)
-    empty = before & (row8 >= 8 - 2 * RIM)
+    empty = after & (row8 < 2 * RIM)
     seam_before = before & (row8 < 2 * RIM) & ((y < last_y) | (row8 < RIM))
     seam_after = after & (row8 < 2 * RIM) & ((y > 0) | (row8 >= RIM))
-    per_slot = jnp.where(before, 1.0 / (bins - 2 * RIM), 1.0 / bins)
+    per_slot = jnp.where(after, 1.0 / (bins - 2 * RIM), 1.0 / bins)
 
     def stratum(k, carry):
         wider, centre = half_ref[k] >= 2, ids_ref[k]
-        end = box_of(win_ref, wider, centre)(2, 8)
-        total = total_ref[k][:1] + jnp.sum(jnp.where(empty, 0.0, end), axis=0, keepdims=True)
+        head = box_of(start_ref, wider, centre)(8 - RIM, 8)
+        total = total_ref[k][:1] + jnp.sum(jnp.where(empty, 0.0, head), axis=0, keepdims=True)
         mean = total * per_slot
         square = jnp.zeros((1, maps), F32)
         for at in range(0, bins, 64):
-            size = min(64, ready - at)
-            part = sums_ref[k, pl.ds(at, size), :]
-            if size < 64:
-                part = jnp.concatenate([part, jnp.where(empty, mean, end)], axis=0)
+            if at == 0:
+                part = [jnp.where(empty, mean, head), sums_ref[k, pl.ds(0, 64 - HEAD), :]]
+                part = jnp.concatenate(part, axis=0)
+            else:
+                part = sums_ref[k, pl.ds(at - HEAD, 64), :]
             part = part - mean
             square = square + jnp.sum(part * part, axis=0, keepdims=True)
             out_ref[k, pl.ds(at, 64), :] = part.astype(BF16)
-        seam = jnp.where(seam_before, pltpu.roll(end, 2 * RIM, axis=0), 0.0)
-        seam = seam + jnp.where(seam_after, box_of(start_ref, wider, centre)(8 - RIM, 8), 0.0)
+        seam = jnp.where(seam_before, box_of(stop_ref, wider, centre)(8 - RIM, 8), 0.0)
+        seam = seam + jnp.where(seam_after, head, 0.0)
         side = jnp.zeros((16, maps), F32)
         for i, value in enumerate(words_of(mean) + words_of(square)):
             side = jnp.where(row == i, value, side)
@@ -238,7 +239,7 @@
     lax.fori_loop(0, strata, stratum, 0, unroll=2)
 
 
-def smoothed(sums, total, first_win, last_win, ahead, stratum_ids, half_width):
+def smoothed(sums, total, first_win, last_win, behind, stratum_ids, half_width):
     strata, ready, maps = sums.shape
     wide = first_win.shape[1]
     smem = pl.BlockSpec(memory_space=pltpu.SMEM)
@@ -247,14 +248,14 @@
         smooth_kernel,
         in_specs=[smem, smem] + [vmem] * 5,
         out_specs=vmem,
-        out_shape=jax.ShapeDtypeStruct((strata, ready + TAIL + 16, maps), BF16),
+        out_shape=jax.ShapeDtypeStruct((strata, ready + HEAD + 16, maps), BF16),
         scratch_shapes=[
             pltpu.VMEM((2, wide, 16, maps), F32),
             pltpu.VMEM((2, wide, 16, maps), F32),
         ],
         compiler_params=params(),
         name="smooth",
-    )(stratum_ids, half_width, sums, total, first_win, last_win, ahead)
+    )(stratum_ids, half_width, sums, total, first_win, last_win, behind)
 
 
 def encode(r):
@@ -295,9 +296,9 @@
         squares.append(sum(square))
         seams.append(sum(seam))
     means = mean_ref[...]
-    short = lax.axis_index("xh") == sum_x - 1
+    short = lax.axis_index("xh") == 0
     b = lax.broadcasted_iota(jnp.int32, (count_blocks, 1), 0)
-    count = jnp.where(short & (b == count_blocks - 1), float(bins - 2 * RIM), float(bins))
+    count = jnp.where(short & (b == 0), float(bins - 2 * RIM), float(bins))
     centre = jnp.sum(means * count, axis=0, keepdims=True)
     centre = centre * jnp.where(short, 1.0 / (count_blocks * bins - 2 * RIM), 1.0 / (count_blocks * bins))
     dev = means - centre
@@ -390,7 +391,7 @@
     means = mean_ref[...]
     row = lax.broadcasted_iota(jnp.int32, (means.shape[0], 1), 0)
     weight = jnp.where(row < parts, float(count), 1.0)
-    weight = jnp.where((row < parts) & (row >= parts - sum_y), float(count - 2 * RIM), weight)
+    weight = jnp.where(row < sum_y, float(count - 2 * RIM), weight)
     dev = means - jnp.sum(means * weight, axis=0, keepdims=True) * (1.0 / total_bins)
     own = jnp.concatenate([squares[m : m + 1] for m in range(panels)], axis=1)
     spread = (own + jnp.sum(dev * dev * weight, axis=0, keepdims=True)) * (1.0 / total_bins)
@@ -482,9 +483,9 @@
     maps, wide, bins = band_maps.shape
     blocks, halves, pairs, sum_y, sum_x = (lax.axis_size(a) for a in ("zl", "zh", "xl", "y", "xh"))
     edge, band_maps = edges(pltpu.with_memory_space_constraint(band_maps, pltpu.HBM))
-    ahead = lax.ppermute(edge, HALO_AXES, next_to_here())
+    behind = lax.ppermute(edge, HALO_AXES, to_next())
     ready = inner(band_maps, stratum_ids, half_width)
-    strata = smoothed(*ready, ahead, stratum_ids, half_width)
+    strata = smoothed(*ready, behind, stratum_ids, half_width)
     strata = lax.all_to_all(strata, STRATA_AXES, 0, 0, tiled=True)
     other = lax.ppermute(strata, "core", [(0, 1), (1, 0)])
     parts = partial_gram(strata, other, blocks, halves, pairs, sum_y, sum_x)

time: 82.2 us -> 81.1 us (0.987)
  starting transfers between devices: 10.9 us -> 6.06 us
  waiting for transfers between devices: 2.38 us -> 7.13 us
  Pallas kernels: 9.46 us -> 8.33 us
    ppermute x1, starting transfers between devices: 8.68 us -> 2.11 us  [body(): behind = lax.ppermute(edge, HALO_AXES, to_next())]
    ppermute x1, waiting for transfers between devices: 0.01 us -> 4.75 us  [body(): behind = lax.ppermute(edge, HALO_AXES, to_next())]
    ppermute x1, starting transfers between devices: 2.2 us -> 3.96 us  [body(): other = lax.ppermute(strata, 'core', [(0, 1), (1, 0)])]
    pallas_call x1, Pallas kernels: 4.26 us -> 3.1 us  [inner(): pl.pallas_call(inner_kernel, in_specs=[smem, smem, vmem], out_specs=[vmem...]
  transfers between devices with their start and end apart: 2 -> 2, of which waited for: 1 -> 2; matrix products, arithmetic and copies ran while one was open for 0% -> 0% of each run, Pallas kernels for 5% -> 4%
where the time goes in v4:
time: 81.1 us; the launch traced here: 80.3 us
  blocking collectives  58.1 us (72%)
  Pallas kernels  8.33 us (10%)
  waiting for transfers between devices  7.13 us (9%)
  starting transfers between devices  6.06 us (7%)
    all_to_all x1, blocking collectives, body(): strata = lax.all_to_all(strata, STRATA_AXES, 0, 0, tiled=True)  32.9 us
    all_to_all x1, blocking collectives, body(): parts = lax.all_to_all(parts, SUM_AXES, 0, 0, tiled=True)  14 us
    all_to_all x1, blocking collectives, body(): tiles = lax.all_to_all(tiles, STRATA_AXES, 0, 0, tiled=True)  11.1 us
    ppermute x1, waiting for transfers between devices, body(): behind = lax.ppermute(edge, HALO_AXES, to_next())  4.75 us
    ppermute x1, starting transfers between devices, body(): other = lax.ppermute(strata, 'core', [(0, 1), (1, 0)])  3.96 us
    pallas_call x1, Pallas kernels, inner(): pl.pallas_call(inner_kernel, in_specs=[smem, smem, vmem], out_specs=[vmem...  3.1 us
    ppermute x1, waiting for transfers between devices, body(): other = lax.ppermute(strata, 'core', [(0, 1), (1, 0)])  2.38 us
    ppermute x1, starting transfers between devices, body(): behind = lax.ppermute(edge, HALO_AXES, to_next())  2.11 us
  transfers between devices with their start and end apart: 2, of which 2 were waited for; matrix products, arithmetic and copies ran while one was open for 0% of the time, Pallas kernels for 4%

profile of v4, /device:TPU:1, one launch (start us, length us, event | category | flops | bytes accessed | tf_op | source)
XLA Modules:
  0.0 80.3 jit_solution(8067624212600277185)
XLA Ops:
  0.6 0.0 copy-start.1
  0.6 0.0 copy-start
  0.6 1.7 %edges.1 = (bf16[128,128]{1,0:T(8,128)(2,1)S(1)}, bf16[128,32,256]{2,1,0:T(8,128)(2,1)S(1)}) custom-call(bf16[128,32,256]{2,1,0:T(8,128)(2,1)} %band_ref.1), custom_call_target="tpu_custom_call" | custom-call | flops 134217728 | bytes 4194304 | tf_op jit(solution)/shard_map/edges/pallas_call | solution.py:66
  2.3 2.1 %collective-permute-start = (bf16[128,128]{1,0:T(8,128)(2,1)S(1)}, bf16[128,128]{1,0:T(8,128)(2,1)S(1)}, u32[]{:S(2)}, u32[]{:S(2)}) collective-permute-start(bf16[128,128]{1,0:T(8,128)(2,1)S(1)} %get-tuple-element.13), channel_id=1, source_target_pairs={{0,4},{4,8},{8,12},{12,16},{16,20},{20,24},{24,28},{28,32},{32,36}... | collective-permute-start | bytes 98312 | tf_op jit(solution)/shard_map/ppermute | solution.py:486
  4.5 0.0 copy-done.1
  4.5 0.0 copy-done
  4.5 3.1 %inner.1 = (f32[16,248,128]{2,1,0:T(8,128)S(1)}, f32[16,8,128]{2,1,0:T(8,128)S(1)}, f32[2,32,8,128]{3,2,1,0:T(8,128)S(1)}, f32[2,32,8,128]{3,2,1,0:T(8,128)S(1)}) custom-call(s32[16]{0:T(128)S(1)} %copy-done, s32[16]{0:T(128)S(1)} %copy-done.1, bf16[128,32,256]{2,1,0:T(8,128)(2,1)S(1)} %get-tuple-element.8.band_ref), custom_call_target="tpu_custom_call" | custom-call | flops 536870912 | bytes 4194304 | tf_op jit(solution)/shard_map/inner/pallas_call | solution.py:157
  7.6 4.8 %collective-permute-done.behind_ref = bf16[128,128]{1,0:T(8,128)(2,1)S(1)} collective-permute-done((bf16[128,128]{1,0:T(8,128)(2,1)S(1)}, bf16[128,128]{1,0:T(8,128)(2,1)S(1)}, u32[]{:S(2)}, u32[]{:S(2)}) %collective-permute-start) | collective-permute-done | bytes 32800 | tf_op jit(solution)/shard_map/ppermute | solution.py:486
  12.3 1.3 %smooth.1 = bf16[16,272,128]{2,1,0:T(8,128)(2,1)S(1)} custom-call(s32[16]{0:T(128)S(1)} %copy-done, s32[16]{0:T(128)S(1)} %copy-done.1, f32[16,248,128]{2,1,0:T(8,128)S(1)} %get-tuple-element.9.sums_ref, f32[16,8,128]{2,1,0:T(8,128)S(1)} %get-tuple-element.10.total_ref, f32[2,32,8,128]{3,2,1,0:T(8,128)S(1)} %get-tuple-element.11.first_win_ref, ...), custom_call_target="tpu_custom_call" | custom-call | tf_op jit(solution)/shard_map/smooth/pallas_call | solution.py:247
  13.6 32.9 %all_to_all.15.refs_0_ = bf16[16,272,128]{2,1,0:T(8,128)(2,1)S(1)} all-to-all(bf16[16,272,128]{2,1,0:T(8,128)(2,1)S(1)} %smooth.1), channel_id=1, replica_groups=mesh['y'=4,'zl'=4,'xh'=2,'xl'=2,'zh'=2,'core'=2] {'zh','zl','xl'}, dimensions={0} | all-to-all | bytes 2228224 | tf_op jit(solution)/shard_map/all_to_all | solution.py:489
  46.5 4.0 %collective-permute-start.1 = (bf16[16,272,128]{2,1,0:T(8,128)(2,1)S(1)}, bf16[16,272,128]{2,1,0:T(8,128)(2,1)S(1)}, u32[]{:S(2)}, u32[]{:S(2)}) collective-permute-start(bf16[16,272,128]{2,1,0:T(8,128)(2,1)S(1)} %all_to_all.15.refs_0_), channel_id=1, source_target_pairs={{0,1},{1,0},{2,3},{3,2},{4,5},{5,4},{6,7},{7,6},{8,9},{9,8},{10,11... | collective-permute-start | bytes 3342344 | tf_op jit(solution)/shard_map/ppermute | solution.py:490
  50.5 2.4 %collective-permute-done.1.refs_1_ = bf16[16,272,128]{2,1,0:T(8,128)(2,1)S(1)} collective-permute-done((bf16[16,272,128]{2,1,0:T(8,128)(2,1)S(1)}, bf16[16,272,128]{2,1,0:T(8,128)(2,1)S(1)}, u32[]{:S(2)}, u32[]{:S(2)}) %collective-permute-start.1) | collective-permute-done | bytes 1114144 | tf_op jit(solution)/shard_map/ppermute | solution.py:490
  52.9 0.9 %partial_gram.1 = bf16[8,192,128]{2,1,0:T(8,128)(2,1)S(1)} custom-call(bf16[16,272,128]{2,1,0:T(8,128)(2,1)S(1)} %all_to_all.15.refs_0_, bf16[16,272,128]{2,1,0:T(8,128)(2,1)S(1)} %collective-permute-done.1.refs_1_), custom_call_target="tpu_custom_call" | custom-call | tf_op jit(solution)/shard_map/partial_gram/pallas_call | solution.py:345
  53.8 14.0 %all_to_all.16.refs_0_ = bf16[8,192,128]{2,1,0:T(8,128)(2,1)S(1)} all-to-all(bf16[8,192,128]{2,1,0:T(8,128)(2,1)S(1)} %partial_gram.1), channel_id=1, replica_groups=mesh['y'=4,'zl'=4,'xh'=2,'xl'=2,'zh'=2,'core'=2] {'xh','y'}, dimensions={0} | all-to-all | bytes 786432 | tf_op jit(solution)/shard_map/all_to_all | solution.py:492
  67.9 0.6 sum_parts.1
  68.5 11.1 %all_to_all.17.in_ref = f32[16,16,128]{2,1,0:T(8,128)S(1)} all-to-all(f32[16,16,128]{2,1,0:T(8,128)S(1)} %sum_parts.1), channel_id=1, replica_groups=mesh['y'=4,'zl'=4,'xh'=2,'xl'=2,'zh'=2,'core'=2] {'zh','zl','xl'}, dimensions={0} | all-to-all | bytes 262144 | tf_op jit(solution)/shard_map/all_to_all | solution.py:494
  79.6 0.7 final.1
Async XLA Ops:
  0.6 3.8 %copy-start.1 = (s32[16]{0:T(128)S(1)}, s32[16]{0:T(128)}, u32[]{:S(2)}) copy-start(s32[16]{0:T(128)} %half_ref.3) | copy-start | bytes 196
  0.6 3.8 %copy-start = (s32[16]{0:T(128)S(1)}, s32[16]{0:T(128)}, u32[]{:S(2)}) copy-start(s32[16]{0:T(128)} %ids_ref.3) | copy-start | bytes 196
  2.3 10.0 %collective-permute-start = (bf16[128,128]{1,0:T(8,128)(2,1)S(1)}, bf16[128,128]{1,0:T(8,128)(2,1)S(1)}, u32[]{:S(2)}, u32[]{:S(2)}) collective-permute-start(bf16[128,128]{1,0:T(8,128)(2,1)S(1)} %get-tuple-element.13), channel_id=1, source_target_pairs={{0,4},{4,8},{8,12},{12,16},{16,20},{20,24},{24,28},{28,32},{32,36}... | collective-permute-start | bytes 98312 | tf_op jit(solution)/shard_map/ppermute | solution.py:486
  46.5 6.3 %collective-permute-start.1 = (bf16[16,272,128]{2,1,0:T(8,128)(2,1)S(1)}, bf16[16,272,128]{2,1,0:T(8,128)(2,1)S(1)}, u32[]{:S(2)}, u32[]{:S(2)}) collective-permute-start(bf16[16,272,128]{2,1,0:T(8,128)(2,1)S(1)} %all_to_all.15.refs_0_), channel_id=1, source_target_pairs={{0,1},{1,0},{2,3},{3,2},{4,5},{5,4},{6,7},{7,6},{8,9},{9,8},{10,11... | collective-permute-start | bytes 3342344 | tf_op jit(solution)/shard_map/ppermute | solution.py:490

commit v5 on v4

--- a/solution.py
+++ b/solution.py
@@ -10,7 +10,7 @@
 BINS_AXES = ("y", "zl") + X_AXES
 MAPS_AXES = ("zh", "core")
 HALO_AXES = BINS_AXES + ("zh",)
-STRATA_AXES = ("zh", "zl", "xl")
+STRATA_AXES = ("zh", "xl", "zl")
 SUM_AXES = ("xh", "y")
 F32 = jnp.float32
 BF16 = jnp.bfloat16
@@ -23,7 +23,7 @@
 
 
 def place(zh, zl, xl, blocks, pairs):
-    return (zh * blocks + zl) * pairs + xl
+    return (zh * pairs + xl) * blocks + zl
 
 
 def to_next():
@@ -236,7 +236,7 @@
         out_ref[k, pl.ds(bins, 16), :] = side.astype(BF16)
         return carry
 
-    lax.fori_loop(0, strata, stratum, 0, unroll=2)
+    lax.fori_loop(0, strata, stratum, 0, unroll=4)
 
 
 def smoothed(sums, total, first_win, last_win, behind, stratum_ids, half_width):

time: 81.1 us -> 79.9 us (0.985)
  blocking collectives: 58.1 us -> 55.8 us
    all_to_all x1, blocking collectives: 32.9 us -> 31.7 us  [body(): strata = lax.all_to_all(strata, STRATA_AXES, 0, 0, tiled=True)]
    all_to_all x1, blocking collectives: 11.1 us -> 10.1 us  [body(): tiles = lax.all_to_all(tiles, STRATA_AXES, 0, 0, tiled=True)]
where the time goes in v5:
time: 79.9 us; the launch traced here: 78.7 us
  blocking collectives  55.8 us (70%)
  Pallas kernels  8.21 us (10%)
  waiting for transfers between devices  7.13 us (9%)
  starting transfers between devices  6.84 us (9%)
    all_to_all x1, blocking collectives, body(): strata = lax.all_to_all(strata, STRATA_AXES, 0, 0, tiled=True)  31.7 us
    all_to_all x1, blocking collectives, body(): parts = lax.all_to_all(parts, SUM_AXES, 0, 0, tiled=True)  14 us
    all_to_all x1, blocking collectives, body(): tiles = lax.all_to_all(tiles, STRATA_AXES, 0, 0, tiled=True)  10.1 us
    ppermute x1, waiting for transfers between devices, body(): behind = lax.ppermute(edge, HALO_AXES, to_next())  4.75 us
    ppermute x1, starting transfers between devices, body(): other = lax.ppermute(strata, 'core', [(0, 1), (1, 0)])  4.74 us
    pallas_call x1, Pallas kernels, inner(): pl.pallas_call(inner_kernel, in_specs=[smem, smem, vmem], out_specs=[vmem...  3.1 us
    ppermute x1, waiting for transfers between devices, body(): other = lax.ppermute(strata, 'core', [(0, 1), (1, 0)])  2.38 us
    ppermute x1, starting transfers between devices, body(): behind = lax.ppermute(edge, HALO_AXES, to_next())  2.11 us
  transfers between devices with their start and end apart: 2, of which 2 were waited for; matrix products, arithmetic and copies ran while one was open for 0% of the time, Pallas kernels for 4%

profile of v5, /device:TPU:1, one launch (start us, length us, event | category | flops | bytes accessed | tf_op | source)
XLA Modules:
  0.0 78.7 jit_solution(5253843979730934355)
XLA Ops:
  0.6 0.0 copy-start.1
  0.6 0.0 copy-start
  0.6 1.7 %edges.1 = (bf16[128,128]{1,0:T(8,128)(2,1)S(1)}, bf16[128,32,256]{2,1,0:T(8,128)(2,1)S(1)}) custom-call(bf16[128,32,256]{2,1,0:T(8,128)(2,1)} %band_ref.1), custom_call_target="tpu_custom_call" | custom-call | flops 134217728 | bytes 4194304 | tf_op jit(solution)/shard_map/edges/pallas_call | solution.py:66
  2.3 2.1 %collective-permute-start = (bf16[128,128]{1,0:T(8,128)(2,1)S(1)}, bf16[128,128]{1,0:T(8,128)(2,1)S(1)}, u32[]{:S(2)}, u32[]{:S(2)}) collective-permute-start(bf16[128,128]{1,0:T(8,128)(2,1)S(1)} %get-tuple-element.13), channel_id=1, source_target_pairs={{0,4},{4,8},{8,12},{12,16},{16,20},{20,24},{24,28},{28,32},{32,36}... | collective-permute-start | bytes 98312 | tf_op jit(solution)/shard_map/ppermute | solution.py:486
  4.5 0.0 copy-done.1
  4.5 0.0 copy-done
  4.5 3.1 %inner.1 = (f32[16,248,128]{2,1,0:T(8,128)S(1)}, f32[16,8,128]{2,1,0:T(8,128)S(1)}, f32[2,32,8,128]{3,2,1,0:T(8,128)S(1)}, f32[2,32,8,128]{3,2,1,0:T(8,128)S(1)}) custom-call(s32[16]{0:T(128)S(1)} %copy-done, s32[16]{0:T(128)S(1)} %copy-done.1, bf16[128,32,256]{2,1,0:T(8,128)(2,1)S(1)} %get-tuple-element.8.band_ref), custom_call_target="tpu_custom_call" | custom-call | flops 536870912 | bytes 4194304 | tf_op jit(solution)/shard_map/inner/pallas_call | solution.py:157
  7.6 4.8 %collective-permute-done.behind_ref = bf16[128,128]{1,0:T(8,128)(2,1)S(1)} collective-permute-done((bf16[128,128]{1,0:T(8,128)(2,1)S(1)}, bf16[128,128]{1,0:T(8,128)(2,1)S(1)}, u32[]{:S(2)}, u32[]{:S(2)}) %collective-permute-start) | collective-permute-done | bytes 32800 | tf_op jit(solution)/shard_map/ppermute | solution.py:486
  12.3 1.2 %smooth.1 = bf16[16,272,128]{2,1,0:T(8,128)(2,1)S(1)} custom-call(s32[16]{0:T(128)S(1)} %copy-done, s32[16]{0:T(128)S(1)} %copy-done.1, f32[16,248,128]{2,1,0:T(8,128)S(1)} %get-tuple-element.9.sums_ref, f32[16,8,128]{2,1,0:T(8,128)S(1)} %get-tuple-element.10.total_ref, f32[2,32,8,128]{3,2,1,0:T(8,128)S(1)} %get-tuple-element.11.first_win_ref, ...), custom_call_target="tpu_custom_call" | custom-call | tf_op jit(solution)/shard_map/smooth/pallas_call | solution.py:247
  13.5 31.7 %all_to_all.15.refs_0_ = bf16[16,272,128]{2,1,0:T(8,128)(2,1)S(1)} all-to-all(bf16[16,272,128]{2,1,0:T(8,128)(2,1)S(1)} %smooth.1), channel_id=1, replica_groups=mesh['y'=4,'zl'=4,'xh'=2,'xl'=2,'zh'=2,'core'=2] {'zh','xl','zl'}, dimensions={0} | all-to-all | bytes 2228224 | tf_op jit(solution)/shard_map/all_to_all | solution.py:489
  45.2 4.7 %collective-permute-start.1 = (bf16[16,272,128]{2,1,0:T(8,128)(2,1)S(1)}, bf16[16,272,128]{2,1,0:T(8,128)(2,1)S(1)}, u32[]{:S(2)}, u32[]{:S(2)}) collective-permute-start(bf16[16,272,128]{2,1,0:T(8,128)(2,1)S(1)} %all_to_all.15.refs_0_), channel_id=1, source_target_pairs={{0,1},{1,0},{2,3},{3,2},{4,5},{5,4},{6,7},{7,6},{8,9},{9,8},{10,11... | collective-permute-start | bytes 3342344 | tf_op jit(solution)/shard_map/ppermute | solution.py:490
  49.9 2.4 %collective-permute-done.1.refs_1_ = bf16[16,272,128]{2,1,0:T(8,128)(2,1)S(1)} collective-permute-done((bf16[16,272,128]{2,1,0:T(8,128)(2,1)S(1)}, bf16[16,272,128]{2,1,0:T(8,128)(2,1)S(1)}, u32[]{:S(2)}, u32[]{:S(2)}) %collective-permute-start.1) | collective-permute-done | bytes 1114144 | tf_op jit(solution)/shard_map/ppermute | solution.py:490
  52.3 0.9 %partial_gram.1 = bf16[8,192,128]{2,1,0:T(8,128)(2,1)S(1)} custom-call(bf16[16,272,128]{2,1,0:T(8,128)(2,1)S(1)} %all_to_all.15.refs_0_, bf16[16,272,128]{2,1,0:T(8,128)(2,1)S(1)} %collective-permute-done.1.refs_1_), custom_call_target="tpu_custom_call" | custom-call | tf_op jit(solution)/shard_map/partial_gram/pallas_call | solution.py:345
  53.3 14.0 %all_to_all.16.refs_0_ = bf16[8,192,128]{2,1,0:T(8,128)(2,1)S(1)} all-to-all(bf16[8,192,128]{2,1,0:T(8,128)(2,1)S(1)} %partial_gram.1), channel_id=1, replica_groups=mesh['y'=4,'zl'=4,'xh'=2,'xl'=2,'zh'=2,'core'=2] {'xh','y'}, dimensions={0} | all-to-all | bytes 786432 | tf_op jit(solution)/shard_map/all_to_all | solution.py:492
  67.3 0.6 sum_parts.1
  67.9 10.1 %all_to_all.17.in_ref = f32[16,16,128]{2,1,0:T(8,128)S(1)} all-to-all(f32[16,16,128]{2,1,0:T(8,128)S(1)} %sum_parts.1), channel_id=1, replica_groups=mesh['y'=4,'zl'=4,'xh'=2,'xl'=2,'zh'=2,'core'=2] {'zh','xl','zl'}, dimensions={0} | all-to-all | bytes 262144 | tf_op jit(solution)/shard_map/all_to_all | solution.py:494
  78.0 0.7 final.1
Async XLA Ops:
  0.6 3.8 %copy-start.1 = (s32[16]{0:T(128)S(1)}, s32[16]{0:T(128)}, u32[]{:S(2)}) copy-start(s32[16]{0:T(128)} %half_ref.3) | copy-start | bytes 196
  0.6 3.8 %copy-start = (s32[16]{0:T(128)S(1)}, s32[16]{0:T(128)}, u32[]{:S(2)}) copy-start(s32[16]{0:T(128)} %ids_ref.3) | copy-start | bytes 196
  2.3 10.0 %collective-permute-start = (bf16[128,128]{1,0:T(8,128)(2,1)S(1)}, bf16[128,128]{1,0:T(8,128)(2,1)S(1)}, u32[]{:S(2)}, u32[]{:S(2)}) collective-permute-start(bf16[128,128]{1,0:T(8,128)(2,1)S(1)} %get-tuple-element.13), channel_id=1, source_target_pairs={{0,4},{4,8},{8,12},{12,16},{16,20},{20,24},{24,28},{28,32},{32,36}... | collective-permute-start | bytes 98312 | tf_op jit(solution)/shard_map/ppermute | solution.py:486
  45.2 7.1 %collective-permute-start.1 = (bf16[16,272,128]{2,1,0:T(8,128)(2,1)S(1)}, bf16[16,272,128]{2,1,0:T(8,128)(2,1)S(1)}, u32[]{:S(2)}, u32[]{:S(2)}) collective-permute-start(bf16[16,272,128]{2,1,0:T(8,128)(2,1)S(1)} %all_to_all.15.refs_0_), channel_id=1, source_target_pairs={{0,1},{1,0},{2,3},{3,2},{4,5},{5,4},{6,7},{7,6},{8,9},{9,8},{10,11... | collective-permute-start | bytes 3342344 | tf_op jit(solution)/shard_map/ppermute | solution.py:490

commit v6 on v5

--- a/solution.py
+++ b/solution.py
@@ -274,12 +274,48 @@
     )
 
 
-def gram_kernel(blocks, halves, pairs, sum_y, sum_x, bins, own_ref, other_ref, out_ref, data_ref, mean_ref, gram_ref):
+TN = (((0,), (0,)), ((), ()))
+
+
+def gather_panels(in_ref, data_ref, blocks, halves, pairs, bins):
+    for m in range(halves):
+        for z in range(blocks):
+            for x in range(pairs):
+                src = place(m, z, x, blocks, pairs)
+                rows = pl.ds((z * pairs + x) * bins, bins)
+                data_ref[rows, pl.ds(m * 128, 128)] = in_ref[src, pl.ds(0, bins), :]
+
+
+def own_kernel(blocks, halves, pairs, bins, own_ref, data_ref, gram_ref):
+    gather_panels(own_ref, data_ref, blocks, halves, pairs, bins)
+    data = data_ref[...]
+    gram_ref[...] = lax.dot_general(data, data, TN, preferred_element_type=F32)
+
+
+def own_gram(own, blocks, halves, pairs):
+    bins = own.shape[1] - 16
+    rows, mine = blocks * pairs * bins, halves * 128
+    vmem = pl.BlockSpec(memory_space=pltpu.VMEM)
+    return pl.pallas_call(
+        lambda *refs: own_kernel(blocks, halves, pairs, bins, *refs),
+        in_specs=[vmem],
+        out_specs=[vmem, vmem],
+        out_shape=[jax.ShapeDtypeStruct((rows, mine), BF16), jax.ShapeDtypeStruct((mine, mine), F32)],
+        compiler_params=params(),
+        cost_estimate=pl.CostEstimate(flops=2 * rows * mine * mine, bytes_accessed=2**21, transcendentals=0),
+        name="own_gram",
+    )(own)
+
+
+def gram_kernel(
+    blocks, halves, pairs, sum_y, sum_x, bins, own_ref, other_ref, mine_ref, square_ref, out_ref, data_ref, mean_ref, gram_ref
+):
     maps = 128
     panels = 2 * halves
     total = panels * maps
     mine = halves * maps
     count_blocks = blocks * pairs
+    gather_panels(other_ref, data_ref, blocks, halves, pairs, bins)
     squares, seams = [], []
     for m in range(panels):
         in_ref = (own_ref, other_ref)[m // halves]
@@ -288,7 +324,6 @@
             for x in range(pairs):
                 src = place(m % halves, z, x, blocks, pairs)
                 b = z * pairs + x
-                data_ref[pl.ds(b * bins, bins), pl.ds(m * maps, maps)] = in_ref[src, pl.ds(0, bins), :]
                 words = in_ref[src, pl.ds(bins, 16), :].astype(F32)
                 mean_ref[b : b + 1, m * maps : (m + 1) * maps] = words[0:1] + words[1:2] + words[2:3]
                 square.append(words[3:4] + words[4:5] + words[5:6])
@@ -308,10 +343,11 @@
     left = [left_hi, left_hi, left_mid, left_mid, left_hi, left_low, jnp.zeros((pad, total), F32)]
     right = [hi, mid, hi, mid, low, hi, jnp.zeros((pad, mine), F32)]
     left, right = (jnp.concatenate(a, axis=0).astype(BF16) for a in (left, right))
-    tn = (((0,), (0,)), ((), ()))
-    gram_ref[...] = lax.dot_general(
-        data_ref[...], data_ref[:, :mine], tn, preferred_element_type=F32
-    ) + lax.dot_general(left, right, tn, preferred_element_type=F32)
+    between = lax.dot_general(left, right, TN, preferred_element_type=F32)
+    gram_ref[:mine] = square_ref[...] + between[:mine]
+    gram_ref[mine:] = between[mine:] + lax.dot_general(
+        data_ref[...], mine_ref[...], TN, preferred_element_type=F32
+    )
     squares = jnp.concatenate(squares, axis=1) + jnp.sum(dev * dev * count, axis=0, keepdims=True)
     by_lane = jnp.where(squares > 0.0, lax.rsqrt(squares), 0.0)
 
@@ -337,24 +373,24 @@
         out_ref[d, pl.ds(halves * blocks * per, SIDE), :] = side
 
 
-def partial_gram(own, other, blocks, halves, pairs, sum_y, sum_x):
+def partial_gram(own, other, mine, square, blocks, halves, pairs, sum_y, sum_x):
     bins = own.shape[1] - 16
     total = 2 * halves * 128
     per = 128 // (blocks * sum_x)
     vmem = pl.BlockSpec(memory_space=pltpu.VMEM)
     return pl.pallas_call(
         lambda *refs: gram_kernel(blocks, halves, pairs, sum_y, sum_x, bins, *refs),
-        in_specs=[vmem, vmem],
+        in_specs=[vmem] * 4,
         out_specs=vmem,
         out_shape=jax.ShapeDtypeStruct((sum_y * sum_x, halves * blocks * per + SIDE, 128), BF16),
         scratch_shapes=[
-            pltpu.VMEM((blocks * pairs * bins, total), BF16),
+            pltpu.VMEM((blocks * pairs * bins, total // 2), BF16),
             pltpu.VMEM((blocks * pairs, total), F32),
             pltpu.VMEM((total, total // 2), F32),
         ],
         compiler_params=params(),
         name="partial_gram",
-    )(own, other)
+    )(own, other, mine, square)
 
 
 def sum_kernel(
@@ -488,7 +524,8 @@
     strata = smoothed(*ready, behind, stratum_ids, half_width)
     strata = lax.all_to_all(strata, STRATA_AXES, 0, 0, tiled=True)
     other = lax.ppermute(strata, "core", [(0, 1), (1, 0)])
-    parts = partial_gram(strata, other, blocks, halves, pairs, sum_y, sum_x)
+    own = own_gram(strata, blocks, halves, pairs)
+    parts = partial_gram(strata, other, *own, blocks, halves, pairs, sum_y, sum_x)
     parts = lax.all_to_all(parts, SUM_AXES, 0, 0, tiled=True)
     tiles = summed(parts, blocks, halves, pairs, sum_y, sum_x, blocks * pairs * bins)
     tiles = lax.all_to_all(tiles, STRATA_AXES, 0, 0, tiled=True)

time: 79.9 us -> 79.6 us (level)
  transfers between devices with their start and end apart: 2 -> 2, of which waited for: 2 -> 2; matrix products, arithmetic and copies ran while one was open for 0% -> 0% of each run, Pallas kernels for 4% -> 5%
where the time goes in v6:
time: 79.6 us; the launch traced here: 78.4 us
  blocking collectives  55.8 us (70%)
  Pallas kernels  8.46 us (11%)
  starting transfers between devices  6.84 us (9%)
  waiting for transfers between devices  6.56 us (8%)
    all_to_all x1, blocking collectives, body(): strata = lax.all_to_all(strata, STRATA_AXES, 0, 0, tiled=True)  31.7 us
    all_to_all x1, blocking collectives, body(): parts = lax.all_to_all(parts, SUM_AXES, 0, 0, tiled=True)  14 us
    all_to_all x1, blocking collectives, body(): tiles = lax.all_to_all(tiles, STRATA_AXES, 0, 0, tiled=True)  10.1 us
    ppermute x1, waiting for transfers between devices, body(): behind = lax.ppermute(edge, HALO_AXES, to_next())  4.75 us
    ppermute x1, starting transfers between devices, body(): other = lax.ppermute(strata, 'core', [(0, 1), (1, 0)])  4.74 us
    pallas_call x1, Pallas kernels, inner(): pl.pallas_call(inner_kernel, in_specs=[smem, smem, vmem], out_specs=[vmem...  3.1 us
    ppermute x1, starting transfers between devices, body(): behind = lax.ppermute(edge, HALO_AXES, to_next())  2.11 us
    ppermute x1, waiting for transfers between devices, body(): other = lax.ppermute(strata, 'core', [(0, 1), (1, 0)])  1.81 us
  transfers between devices with their start and end apart: 2, of which 2 were waited for; matrix products, arithmetic and copies ran while one was open for 0% of the time, Pallas kernels for 5%

profile of v6, /device:TPU:1, one launch (start us, length us, event | category | flops | bytes accessed | tf_op | source)
XLA Modules:
  0.0 78.4 jit_solution(5408499912807096467)
XLA Ops:
  0.6 0.0 copy-start.1
  0.6 0.0 copy-start
  0.6 1.7 %edges.1 = (bf16[128,128]{1,0:T(8,128)(2,1)S(1)}, bf16[128,32,256]{2,1,0:T(8,128)(2,1)S(1)}) custom-call(bf16[128,32,256]{2,1,0:T(8,128)(2,1)} %band_ref.1), custom_call_target="tpu_custom_call" | custom-call | flops 134217728 | bytes 4194304 | tf_op jit(solution)/shard_map/edges/pallas_call | solution.py:66
  2.3 2.1 %collective-permute-start = (bf16[128,128]{1,0:T(8,128)(2,1)S(1)}, bf16[128,128]{1,0:T(8,128)(2,1)S(1)}, u32[]{:S(2)}, u32[]{:S(2)}) collective-permute-start(bf16[128,128]{1,0:T(8,128)(2,1)S(1)} %get-tuple-element.15), channel_id=1, source_target_pairs={{0,4},{4,8},{8,12},{12,16},{16,20},{20,24},{24,28},{28,32},{32,36}... | collective-permute-start | bytes 98312 | tf_op jit(solution)/shard_map/ppermute | solution.py:522
  4.5 0.0 copy-done.1
  4.5 0.0 copy-done
  4.5 3.1 %inner.1 = (f32[16,248,128]{2,1,0:T(8,128)S(1)}, f32[16,8,128]{2,1,0:T(8,128)S(1)}, f32[2,32,8,128]{3,2,1,0:T(8,128)S(1)}, f32[2,32,8,128]{3,2,1,0:T(8,128)S(1)}) custom-call(s32[16]{0:T(128)S(1)} %copy-done, s32[16]{0:T(128)S(1)} %copy-done.1, bf16[128,32,256]{2,1,0:T(8,128)(2,1)S(1)} %get-tuple-element.10.band_ref), custom_call_target="tpu_custom_call" | custom-call | flops 536870912 | bytes 4194304 | tf_op jit(solution)/shard_map/inner/pallas_call | solution.py:157
  7.6 4.8 %collective-permute-done.behind_ref = bf16[128,128]{1,0:T(8,128)(2,1)S(1)} collective-permute-done((bf16[128,128]{1,0:T(8,128)(2,1)S(1)}, bf16[128,128]{1,0:T(8,128)(2,1)S(1)}, u32[]{:S(2)}, u32[]{:S(2)}) %collective-permute-start) | collective-permute-done | bytes 32800 | tf_op jit(solution)/shard_map/ppermute | solution.py:522
  12.3 1.2 %smooth.1 = bf16[16,272,128]{2,1,0:T(8,128)(2,1)S(1)} custom-call(s32[16]{0:T(128)S(1)} %copy-done, s32[16]{0:T(128)S(1)} %copy-done.1, f32[16,248,128]{2,1,0:T(8,128)S(1)} %get-tuple-element.11.sums_ref, f32[16,8,128]{2,1,0:T(8,128)S(1)} %get-tuple-element.12.total_ref, f32[2,32,8,128]{3,2,1,0:T(8,128)S(1)} %get-tuple-element.13.first_win_ref, ...), custom_call_target="tpu_custom_call" | custom-call | tf_op jit(solution)/shard_map/smooth/pallas_call | solution.py:247
  13.5 31.7 %all_to_all.15.refs_0_ = bf16[16,272,128]{2,1,0:T(8,128)(2,1)S(1)} all-to-all(bf16[16,272,128]{2,1,0:T(8,128)(2,1)S(1)} %smooth.1), channel_id=1, replica_groups=mesh['y'=4,'zl'=4,'xh'=2,'xl'=2,'zh'=2,'core'=2] {'zh','xl','zl'}, dimensions={0} | all-to-all | bytes 2228224 | tf_op jit(solution)/shard_map/all_to_all | solution.py:525
  45.2 4.7 %collective-permute-start.1 = (bf16[16,272,128]{2,1,0:T(8,128)(2,1)S(1)}, bf16[16,272,128]{2,1,0:T(8,128)(2,1)S(1)}, u32[]{:S(2)}, u32[]{:S(2)}) collective-permute-start(bf16[16,272,128]{2,1,0:T(8,128)(2,1)S(1)} %all_to_all.15.refs_0_), channel_id=1, source_target_pairs={{0,1},{1,0},{2,3},{3,2},{4,5},{5,4},{6,7},{7,6},{8,9},{9,8},{10,11... | collective-permute-start | bytes 3342344 | tf_op jit(solution)/shard_map/ppermute | solution.py:526
  49.9 0.6 own_gram.1
  50.5 1.8 %collective-permute-done.1.refs_1_ = bf16[16,272,128]{2,1,0:T(8,128)(2,1)S(1)} collective-permute-done((bf16[16,272,128]{2,1,0:T(8,128)(2,1)S(1)}, bf16[16,272,128]{2,1,0:T(8,128)(2,1)S(1)}, u32[]{:S(2)}, u32[]{:S(2)}) %collective-permute-start.1) | collective-permute-done | bytes 1114144 | tf_op jit(solution)/shard_map/ppermute | solution.py:526
  52.3 0.6 partial_gram.1
  53.0 14.0 %all_to_all.16.refs_0_ = bf16[8,192,128]{2,1,0:T(8,128)(2,1)S(1)} all-to-all(bf16[8,192,128]{2,1,0:T(8,128)(2,1)S(1)} %partial_gram.1), channel_id=1, replica_groups=mesh['y'=4,'zl'=4,'xh'=2,'xl'=2,'zh'=2,'core'=2] {'xh','y'}, dimensions={0} | all-to-all | bytes 786432 | tf_op jit(solution)/shard_map/all_to_all | solution.py:529
  67.0 0.6 sum_parts.1
  67.6 10.1 %all_to_all.17.in_ref = f32[16,16,128]{2,1,0:T(8,128)S(1)} all-to-all(f32[16,16,128]{2,1,0:T(8,128)S(1)} %sum_parts.1), channel_id=1, replica_groups=mesh['y'=4,'zl'=4,'xh'=2,'xl'=2,'zh'=2,'core'=2] {'zh','xl','zl'}, dimensions={0} | all-to-all | bytes 262144 | tf_op jit(solution)/shard_map/all_to_all | solution.py:531
  77.7 0.7 final.1
Async XLA Ops:
  0.6 3.8 %copy-start.1 = (s32[16]{0:T(128)S(1)}, s32[16]{0:T(128)}, u32[]{:S(2)}) copy-start(s32[16]{0:T(128)} %half_ref.3) | copy-start | bytes 196
  0.6 3.8 %copy-start = (s32[16]{0:T(128)S(1)}, s32[16]{0:T(128)}, u32[]{:S(2)}) copy-start(s32[16]{0:T(128)} %ids_ref.3) | copy-start | bytes 196
  2.3 10.0 %collective-permute-start = (bf16[128,128]{1,0:T(8,128)(2,1)S(1)}, bf16[128,128]{1,0:T(8,128)(2,1)S(1)}, u32[]{:S(2)}, u32[]{:S(2)}) collective-permute-start(bf16[128,128]{1,0:T(8,128)(2,1)S(1)} %get-tuple-element.15), channel_id=1, source_target_pairs={{0,4},{4,8},{8,12},{12,16},{16,20},{20,24},{24,28},{28,32},{32,36}... | collective-permute-start | bytes 98312 | tf_op jit(solution)/shard_map/ppermute | solution.py:522
  45.2 7.1 %collective-permute-start.1 = (bf16[16,272,128]{2,1,0:T(8,128)(2,1)S(1)}, bf16[16,272,128]{2,1,0:T(8,128)(2,1)S(1)}, u32[]{:S(2)}, u32[]{:S(2)}) collective-permute-start(bf16[16,272,128]{2,1,0:T(8,128)(2,1)S(1)} %all_to_all.15.refs_0_), channel_id=1, source_target_pairs={{0,1},{1,0},{2,3},{3,2},{4,5},{5,4},{6,7},{7,6},{8,9},{9,8},{10,11... | collective-permute-start | bytes 3342344 | tf_op jit(solution)/shard_map/ppermute | solution.py:526

commit v7 on v6

--- a/solution.py
+++ b/solution.py
@@ -17,7 +17,7 @@
 HALO = 4
 HEAD = 8
 RIM = 2
-SIDE = 64
+SIDE = 48
 SPAN = 200.0
 VMEM_LIMIT = 28 * 1024 * 1024
 
@@ -266,6 +266,12 @@
 def decode(code):
     size = jnp.log2(jnp.abs(code)) * (1.0 / SPAN) + 0.5
     return jnp.where(code < 0.0, -size, size)
+
+
+def share(left, rows):
+    bin = lax.rem(lax.broadcasted_iota(jnp.int32, (rows, 128), 0), 2 * RIM).astype(F32)
+    part = 0.9 - bin * (0.8 / (2 * RIM - 1))
+    return jnp.where(left, part, 1.0 - part)
 
 
 def dot_tn(a, b):
@@ -354,8 +360,12 @@
     def rows_of(line):
         return jnp.concatenate([line[:, m * maps : (m + 1) * maps] for m in range(panels)], axis=0)
 
-    side = words_of(rows_of(centre)) + words_of(rows_of(squares)) + words_of(jnp.concatenate(seams, axis=0))[:2]
-    side += (jnp.zeros((SIDE - (6 + 4 * RIM) * panels, maps), F32),)
+    of_mean = jnp.concatenate(
+        [jnp.broadcast_to(centre[:, m * maps : (m + 1) * maps], (2 * RIM, maps)) for m in range(panels)], axis=0
+    )
+    seam = jnp.concatenate(seams, axis=0) - share(lax.axis_index("xh") == sum_x - 1, 2 * RIM * panels) * of_mean
+    side = words_of(rows_of(centre)) + words_of(rows_of(squares)) + (seam,)
+    side += (jnp.zeros((SIDE - (6 + 2 * RIM) * panels, maps), F32),)
     side = jnp.concatenate(side, axis=0).astype(BF16)
     core = lax.axis_index("core")
     per = maps // (blocks * sum_x)
@@ -412,7 +422,10 @@
             for i in (0, 3 * panels)
         )
         size = 2 * RIM * panels
-        seams.append(side[6 * panels : 6 * panels + size] + side[6 * panels + size : 6 * panels + 2 * size])
+        of_mean = jnp.concatenate(
+            [jnp.broadcast_to(mean[m : m + 1], (2 * RIM, maps)) for m in range(panels)], axis=0
+        )
+        seams.append(side[6 * panels : 6 * panels + size] + share(d >= parts - sum_y, size) * of_mean)
         squares = squares + square
         scale = jnp.sqrt(square)
         for m in range(panels):

time: 79.6 us -> 79.2 us (level)
  no operation moved by 1% of the time
where the time goes in v7:
time: 79.2 us; the launch traced here: 78.2 us
  blocking collectives  55.6 us (70%)
  Pallas kernels  8.48 us (11%)
  starting transfers between devices  6.84 us (9%)
  waiting for transfers between devices  6.56 us (8%)
    all_to_all x1, blocking collectives, body(): strata = lax.all_to_all(strata, STRATA_AXES, 0, 0, tiled=True)  31.7 us
    all_to_all x1, blocking collectives, body(): parts = lax.all_to_all(parts, SUM_AXES, 0, 0, tiled=True)  13.8 us
    all_to_all x1, blocking collectives, body(): tiles = lax.all_to_all(tiles, STRATA_AXES, 0, 0, tiled=True)  10.1 us
    ppermute x1, waiting for transfers between devices, body(): behind = lax.ppermute(edge, HALO_AXES, to_next())  4.75 us
    ppermute x1, starting transfers between devices, body(): other = lax.ppermute(strata, 'core', [(0, 1), (1, 0)])  4.74 us
    pallas_call x1, Pallas kernels, inner(): pl.pallas_call(inner_kernel, in_specs=[smem, smem, vmem], out_specs=[vmem...  3.1 us
    ppermute x1, starting transfers between devices, body(): behind = lax.ppermute(edge, HALO_AXES, to_next())  2.11 us
    ppermute x1, waiting for transfers between devices, body(): other = lax.ppermute(strata, 'core', [(0, 1), (1, 0)])  1.81 us
  transfers between devices with their start and end apart: 2, of which 2 were waited for; matrix products, arithmetic and copies ran while one was open for 0% of the time, Pallas kernels for 5%

profile of v7, /device:TPU:1, one launch (start us, length us, event | category | flops | bytes accessed | tf_op | source)
XLA Modules:
  0.0 78.2 jit_solution(17444114669551175807)
XLA Ops:
  0.6 0.0 copy-start.1
  0.6 0.0 copy-start
  0.6 1.7 %edges.1 = (bf16[128,128]{1,0:T(8,128)(2,1)S(1)}, bf16[128,32,256]{2,1,0:T(8,128)(2,1)S(1)}) custom-call(bf16[128,32,256]{2,1,0:T(8,128)(2,1)} %band_ref.1), custom_call_target="tpu_custom_call" | custom-call | flops 134217728 | bytes 4194304 | tf_op jit(solution)/shard_map/edges/pallas_call | solution.py:66
  2.3 2.1 %collective-permute-start = (bf16[128,128]{1,0:T(8,128)(2,1)S(1)}, bf16[128,128]{1,0:T(8,128)(2,1)S(1)}, u32[]{:S(2)}, u32[]{:S(2)}) collective-permute-start(bf16[128,128]{1,0:T(8,128)(2,1)S(1)} %get-tuple-element.15), channel_id=1, source_target_pairs={{0,4},{4,8},{8,12},{12,16},{16,20},{20,24},{24,28},{28,32},{32,36}... | collective-permute-start | bytes 98312 | tf_op jit(solution)/shard_map/ppermute | solution.py:535
  4.5 0.0 copy-done.1
  4.5 0.0 copy-done
  4.5 3.1 %inner.1 = (f32[16,248,128]{2,1,0:T(8,128)S(1)}, f32[16,8,128]{2,1,0:T(8,128)S(1)}, f32[2,32,8,128]{3,2,1,0:T(8,128)S(1)}, f32[2,32,8,128]{3,2,1,0:T(8,128)S(1)}) custom-call(s32[16]{0:T(128)S(1)} %copy-done, s32[16]{0:T(128)S(1)} %copy-done.1, bf16[128,32,256]{2,1,0:T(8,128)(2,1)S(1)} %get-tuple-element.10.band_ref), custom_call_target="tpu_custom_call" | custom-call | flops 536870912 | bytes 4194304 | tf_op jit(solution)/shard_map/inner/pallas_call | solution.py:157
  7.6 4.8 %collective-permute-done.behind_ref = bf16[128,128]{1,0:T(8,128)(2,1)S(1)} collective-permute-done((bf16[128,128]{1,0:T(8,128)(2,1)S(1)}, bf16[128,128]{1,0:T(8,128)(2,1)S(1)}, u32[]{:S(2)}, u32[]{:S(2)}) %collective-permute-start) | collective-permute-done | bytes 32800 | tf_op jit(solution)/shard_map/ppermute | solution.py:535
  12.3 1.2 %smooth.1 = bf16[16,272,128]{2,1,0:T(8,128)(2,1)S(1)} custom-call(s32[16]{0:T(128)S(1)} %copy-done, s32[16]{0:T(128)S(1)} %copy-done.1, f32[16,248,128]{2,1,0:T(8,128)S(1)} %get-tuple-element.11.sums_ref, f32[16,8,128]{2,1,0:T(8,128)S(1)} %get-tuple-element.12.total_ref, f32[2,32,8,128]{3,2,1,0:T(8,128)S(1)} %get-tuple-element.13.first_win_ref, ...), custom_call_target="tpu_custom_call" | custom-call | tf_op jit(solution)/shard_map/smooth/pallas_call | solution.py:247
  13.5 31.7 %all_to_all.15.refs_0_ = bf16[16,272,128]{2,1,0:T(8,128)(2,1)S(1)} all-to-all(bf16[16,272,128]{2,1,0:T(8,128)(2,1)S(1)} %smooth.1), channel_id=1, replica_groups=mesh['y'=4,'zl'=4,'xh'=2,'xl'=2,'zh'=2,'core'=2] {'zh','xl','zl'}, dimensions={0} | all-to-all | bytes 2228224 | tf_op jit(solution)/shard_map/all_to_all | solution.py:538
  45.2 4.7 %collective-permute-start.1 = (bf16[16,272,128]{2,1,0:T(8,128)(2,1)S(1)}, bf16[16,272,128]{2,1,0:T(8,128)(2,1)S(1)}, u32[]{:S(2)}, u32[]{:S(2)}) collective-permute-start(bf16[16,272,128]{2,1,0:T(8,128)(2,1)S(1)} %all_to_all.15.refs_0_), channel_id=1, source_target_pairs={{0,1},{1,0},{2,3},{3,2},{4,5},{5,4},{6,7},{7,6},{8,9},{9,8},{10,11... | collective-permute-start | bytes 3342344 | tf_op jit(solution)/shard_map/ppermute | solution.py:539
  49.9 0.6 own_gram.1
  50.5 1.8 %collective-permute-done.1.refs_1_ = bf16[16,272,128]{2,1,0:T(8,128)(2,1)S(1)} collective-permute-done((bf16[16,272,128]{2,1,0:T(8,128)(2,1)S(1)}, bf16[16,272,128]{2,1,0:T(8,128)(2,1)S(1)}, u32[]{:S(2)}, u32[]{:S(2)}) %collective-permute-start.1) | collective-permute-done | bytes 1114144 | tf_op jit(solution)/shard_map/ppermute | solution.py:539
  52.3 0.6 partial_gram.1
  53.0 13.8 %all_to_all.16.refs_0_ = bf16[8,176,128]{2,1,0:T(8,128)(2,1)S(1)} all-to-all(bf16[8,176,128]{2,1,0:T(8,128)(2,1)S(1)} %partial_gram.1), channel_id=1, replica_groups=mesh['y'=4,'zl'=4,'xh'=2,'xl'=2,'zh'=2,'core'=2] {'xh','y'}, dimensions={0} | all-to-all | bytes 720896 | tf_op jit(solution)/shard_map/all_to_all | solution.py:542
  66.8 0.6 sum_parts.1
  67.4 10.1 %all_to_all.17.in_ref = f32[16,16,128]{2,1,0:T(8,128)S(1)} all-to-all(f32[16,16,128]{2,1,0:T(8,128)S(1)} %sum_parts.1), channel_id=1, replica_groups=mesh['y'=4,'zl'=4,'xh'=2,'xl'=2,'zh'=2,'core'=2] {'zh','xl','zl'}, dimensions={0} | all-to-all | bytes 262144 | tf_op jit(solution)/shard_map/all_to_all | solution.py:544
  77.5 0.7 final.1
Async XLA Ops:
  0.6 3.8 %copy-start.1 = (s32[16]{0:T(128)S(1)}, s32[16]{0:T(128)}, u32[]{:S(2)}) copy-start(s32[16]{0:T(128)} %half_ref.3) | copy-start | bytes 196
  0.6 3.8 %copy-start = (s32[16]{0:T(128)S(1)}, s32[16]{0:T(128)}, u32[]{:S(2)}) copy-start(s32[16]{0:T(128)} %ids_ref.3) | copy-start | bytes 196
  2.3 10.0 %collective-permute-start = (bf16[128,128]{1,0:T(8,128)(2,1)S(1)}, bf16[128,128]{1,0:T(8,128)(2,1)S(1)}, u32[]{:S(2)}, u32[]{:S(2)}) collective-permute-start(bf16[128,128]{1,0:T(8,128)(2,1)S(1)} %get-tuple-element.15), channel_id=1, source_target_pairs={{0,4},{4,8},{8,12},{12,16},{16,20},{20,24},{24,28},{28,32},{32,36}... | collective-permute-start | bytes 98312 | tf_op jit(solution)/shard_map/ppermute | solution.py:535
  45.2 7.1 %collective-permute-start.1 = (bf16[16,272,128]{2,1,0:T(8,128)(2,1)S(1)}, bf16[16,272,128]{2,1,0:T(8,128)(2,1)S(1)}, u32[]{:S(2)}, u32[]{:S(2)}) collective-permute-start(bf16[16,272,128]{2,1,0:T(8,128)(2,1)S(1)} %all_to_all.15.refs_0_), channel_id=1, source_target_pairs={{0,1},{1,0},{2,3},{3,2},{4,5},{5,4},{6,7},{7,6},{8,9},{9,8},{10,11... | collective-permute-start | bytes 3342344 | tf_op jit(solution)/shard_map/ppermute | solution.py:539

commit v8 on v7

--- a/solution.py
+++ b/solution.py
@@ -131,15 +131,15 @@
         windows([turned_ref[d, rows, :] for d in range(wide)], win_ref, rows)
         return carry
 
-    lax.fori_loop(0, bins // 16, some, 0)
+    lax.fori_loop(0, bins // 16, some, 0, unroll=2)
     first_win_ref[...] = win_ref[:, :, pl.ds(0, 8), :]
     last_win_ref[...] = win_ref[:, :, pl.ds(bins - 8, 8), :]
 
     def stratum(k, carry):
         box = box_of(win_ref, half_ref[k] >= 2, ids_ref[k])
         total = jnp.zeros((1, maps), F32)
-        for at in range(0, bins - HEAD, 64):
-            size = min(64, bins - HEAD - at)
+        for at in range(0, bins - HEAD, 128):
+            size = min(128, bins - HEAD - at)
             part = box(at + HEAD - RIM, size)
             sums_ref[k, pl.ds(at, size), :] = part
             total = total + jnp.sum(part, axis=0, keepdims=True)

time: 79.2 us -> 79.2 us (level)
  no operation moved by 1% of the time
where the time goes in v8:
time: 79.2 us; the launch traced here: 78.1 us
  blocking collectives  55.5 us (70%)
  Pallas kernels  8.44 us (11%)
  starting transfers between devices  6.84 us (9%)
  waiting for transfers between devices  6.6 us (8%)
    all_to_all x1, blocking collectives, body(): strata = lax.all_to_all(strata, STRATA_AXES, 0, 0, tiled=True)  31.7 us
    all_to_all x1, blocking collectives, body(): parts = lax.all_to_all(parts, SUM_AXES, 0, 0, tiled=True)  13.8 us
    all_to_all x1, blocking collectives, body(): tiles = lax.all_to_all(tiles, STRATA_AXES, 0, 0, tiled=True)  10.1 us
    ppermute x1, waiting for transfers between devices, body(): behind = lax.ppermute(edge, HALO_AXES, to_next())  4.79 us
    ppermute x1, starting transfers between devices, body(): other = lax.ppermute(strata, 'core', [(0, 1), (1, 0)])  4.74 us
    pallas_call x1, Pallas kernels, inner(): pl.pallas_call(inner_kernel, in_specs=[smem, smem, vmem], out_specs=[vmem...  3.06 us
    ppermute x1, starting transfers between devices, body(): behind = lax.ppermute(edge, HALO_AXES, to_next())  2.11 us
    ppermute x1, waiting for transfers between devices, body(): other = lax.ppermute(strata, 'core', [(0, 1), (1, 0)])  1.81 us
  transfers between devices with their start and end apart: 2, of which 2 were waited for; matrix products, arithmetic and copies ran while one was open for 0% of the time, Pallas kernels for 5%

profile of v8, /device:TPU:1, one launch (start us, length us, event | category | flops | bytes accessed | tf_op | source)
XLA Modules:
  0.0 78.1 jit_solution(3341529609410016270)
XLA Ops:
  0.6 0.0 copy-start.1
  0.6 0.0 copy-start
  0.6 1.7 %edges.1 = (bf16[128,128]{1,0:T(8,128)(2,1)S(1)}, bf16[128,32,256]{2,1,0:T(8,128)(2,1)S(1)}) custom-call(bf16[128,32,256]{2,1,0:T(8,128)(2,1)} %band_ref.1), custom_call_target="tpu_custom_call" | custom-call | flops 134217728 | bytes 4194304 | tf_op jit(solution)/shard_map/edges/pallas_call | solution.py:66
  2.3 2.1 %collective-permute-start = (bf16[128,128]{1,0:T(8,128)(2,1)S(1)}, bf16[128,128]{1,0:T(8,128)(2,1)S(1)}, u32[]{:S(2)}, u32[]{:S(2)}) collective-permute-start(bf16[128,128]{1,0:T(8,128)(2,1)S(1)} %get-tuple-element.15), channel_id=1, source_target_pairs={{0,4},{4,8},{8,12},{12,16},{16,20},{20,24},{24,28},{28,32},{32,36}... | collective-permute-start | bytes 98312 | tf_op jit(solution)/shard_map/ppermute | solution.py:535
  4.5 0.0 copy-done.1
  4.5 0.0 copy-done
  4.5 3.1 %inner.1 = (f32[16,248,128]{2,1,0:T(8,128)S(1)}, f32[16,8,128]{2,1,0:T(8,128)S(1)}, f32[2,32,8,128]{3,2,1,0:T(8,128)S(1)}, f32[2,32,8,128]{3,2,1,0:T(8,128)S(1)}) custom-call(s32[16]{0:T(128)S(1)} %copy-done, s32[16]{0:T(128)S(1)} %copy-done.1, bf16[128,32,256]{2,1,0:T(8,128)(2,1)S(1)} %get-tuple-element.10.band_ref), custom_call_target="tpu_custom_call" | custom-call | flops 536870912 | bytes 4194304 | tf_op jit(solution)/shard_map/inner/pallas_call | solution.py:157
  7.5 4.8 %collective-permute-done.behind_ref = bf16[128,128]{1,0:T(8,128)(2,1)S(1)} collective-permute-done((bf16[128,128]{1,0:T(8,128)(2,1)S(1)}, bf16[128,128]{1,0:T(8,128)(2,1)S(1)}, u32[]{:S(2)}, u32[]{:S(2)}) %collective-permute-start) | collective-permute-done | bytes 32800 | tf_op jit(solution)/shard_map/ppermute | solution.py:535
  12.3 1.2 %smooth.1 = bf16[16,272,128]{2,1,0:T(8,128)(2,1)S(1)} custom-call(s32[16]{0:T(128)S(1)} %copy-done, s32[16]{0:T(128)S(1)} %copy-done.1, f32[16,248,128]{2,1,0:T(8,128)S(1)} %get-tuple-element.11.sums_ref, f32[16,8,128]{2,1,0:T(8,128)S(1)} %get-tuple-element.12.total_ref, f32[2,32,8,128]{3,2,1,0:T(8,128)S(1)} %get-tuple-element.13.first_win_ref, ...), custom_call_target="tpu_custom_call" | custom-call | tf_op jit(solution)/shard_map/smooth/pallas_call | solution.py:247
  13.5 31.7 %all_to_all.15.refs_0_ = bf16[16,272,128]{2,1,0:T(8,128)(2,1)S(1)} all-to-all(bf16[16,272,128]{2,1,0:T(8,128)(2,1)S(1)} %smooth.1), channel_id=1, replica_groups=mesh['y'=4,'zl'=4,'xh'=2,'xl'=2,'zh'=2,'core'=2] {'zh','xl','zl'}, dimensions={0} | all-to-all | bytes 2228224 | tf_op jit(solution)/shard_map/all_to_all | solution.py:538
  45.2 4.7 %collective-permute-start.1 = (bf16[16,272,128]{2,1,0:T(8,128)(2,1)S(1)}, bf16[16,272,128]{2,1,0:T(8,128)(2,1)S(1)}, u32[]{:S(2)}, u32[]{:S(2)}) collective-permute-start(bf16[16,272,128]{2,1,0:T(8,128)(2,1)S(1)} %all_to_all.15.refs_0_), channel_id=1, source_target_pairs={{0,1},{1,0},{2,3},{3,2},{4,5},{5,4},{6,7},{7,6},{8,9},{9,8},{10,11... | collective-permute-start | bytes 3342344 | tf_op jit(solution)/shard_map/ppermute | solution.py:539
  49.9 0.6 own_gram.1
  50.5 1.8 %collective-permute-done.1.refs_1_ = bf16[16,272,128]{2,1,0:T(8,128)(2,1)S(1)} collective-permute-done((bf16[16,272,128]{2,1,0:T(8,128)(2,1)S(1)}, bf16[16,272,128]{2,1,0:T(8,128)(2,1)S(1)}, u32[]{:S(2)}, u32[]{:S(2)}) %collective-permute-start.1) | collective-permute-done | bytes 1114144 | tf_op jit(solution)/shard_map/ppermute | solution.py:539
  52.3 0.6 partial_gram.1
  53.0 13.8 %all_to_all.16.refs_0_ = bf16[8,176,128]{2,1,0:T(8,128)(2,1)S(1)} all-to-all(bf16[8,176,128]{2,1,0:T(8,128)(2,1)S(1)} %partial_gram.1), channel_id=1, replica_groups=mesh['y'=4,'zl'=4,'xh'=2,'xl'=2,'zh'=2,'core'=2] {'xh','y'}, dimensions={0} | all-to-all | bytes 720896 | tf_op jit(solution)/shard_map/all_to_all | solution.py:542
  66.7 0.6 sum_parts.1
  67.4 10.1 %all_to_all.17.in_ref = f32[16,16,128]{2,1,0:T(8,128)S(1)} all-to-all(f32[16,16,128]{2,1,0:T(8,128)S(1)} %sum_parts.1), channel_id=1, replica_groups=mesh['y'=4,'zl'=4,'xh'=2,'xl'=2,'zh'=2,'core'=2] {'zh','xl','zl'}, dimensions={0} | all-to-all | bytes 262144 | tf_op jit(solution)/shard_map/all_to_all | solution.py:544
  77.4 0.7 final.1
Async XLA Ops:
  0.6 3.8 %copy-start.1 = (s32[16]{0:T(128)S(1)}, s32[16]{0:T(128)}, u32[]{:S(2)}) copy-start(s32[16]{0:T(128)} %half_ref.3) | copy-start | bytes 196
  0.6 3.8 %copy-start = (s32[16]{0:T(128)S(1)}, s32[16]{0:T(128)}, u32[]{:S(2)}) copy-start(s32[16]{0:T(128)} %ids_ref.3) | copy-start | bytes 196
  2.3 10.0 %collective-permute-start = (bf16[128,128]{1,0:T(8,128)(2,1)S(1)}, bf16[128,128]{1,0:T(8,128)(2,1)S(1)}, u32[]{:S(2)}, u32[]{:S(2)}) collective-permute-start(bf16[128,128]{1,0:T(8,128)(2,1)S(1)} %get-tuple-element.15), channel_id=1, source_target_pairs={{0,4},{4,8},{8,12},{12,16},{16,20},{20,24},{24,28},{28,32},{32,36}... | collective-permute-start | bytes 98312 | tf_op jit(solution)/shard_map/ppermute | solution.py:535
  45.2 7.1 %collective-permute-start.1 = (bf16[16,272,128]{2,1,0:T(8,128)(2,1)S(1)}, bf16[16,272,128]{2,1,0:T(8,128)(2,1)S(1)}, u32[]{:S(2)}, u32[]{:S(2)}) collective-permute-start(bf16[16,272,128]{2,1,0:T(8,128)(2,1)S(1)} %all_to_all.15.refs_0_), channel_id=1, source_target_pairs={{0,1},{1,0},{2,3},{3,2},{4,5},{5,4},{6,7},{7,6},{8,9},{9,8},{10,11... | collective-permute-start | bytes 3342344 | tf_op jit(solution)/shard_map/ppermute | solution.py:539
